TPU v7x, 32 devices: a whole 2x2x4 slice. The times are simulated.
32 devices in a mesh: leaf: 32 (over z, y, x, core).
Axes of the slice: x: 2, y: 2, z: 4, core: 2. Of those that a mesh axis runs over, the one named last changes fastest.
Arguments:
- points: float32 [16, 65536], P(None, 'leaf'), may hold values from -6 to 6
- order: int32 [65536], P('leaf'), may hold values from 0 to 65535, as said below
- bases: float32 [256, 256, 64], P('leaf'), may hold values from -0.375 to 0.375
- lift: float32 [256, 64, 64], P('leaf'), may hold values from -0.25 to 0.25
- near_ids: int32 [256, 3], P('leaf'), may hold values from 0 to 255, as said below
- near_blocks: float32 [256, 3, 256, 256], P('leaf'), may hold values from -0.21875 to 0.21875
- far_ids: int32 [256, 8], P('leaf'), may hold values from 0 to 255, as said below
- far_count: int32 [256], P('leaf'), may hold values from 1 to 8
- far_blocks: float32 [256, 8, 64, 64], P('leaf'), may hold values from -0.25 to 0.25
- transfer: float32 [4, 2, 64, 64], replicated, may hold values from -0.5 to 0.5
- couple: float32 [4, 4, 64, 64], replicated, may hold values from -0.375 to 0.375
- links: int32 [32, 4, 4], P('leaf'), may hold values from 0 to 1, as said below
- top_couple: float32 [64, 64], replicated, may hold values from -0.75 to 0.75
Outputs:
- product: float32 [16, 65536], P(None, 'leaf')
Inputs may be any that keep to these rules, and one draw needn't show every extreme that they name: `order`: each subtree's 2048 entries are a permutation of that subtree's positions. `near_ids`: the first entry of a leaf is the leaf itself; the others lie at most one leaf away. `far_ids`: a coupled leaf lies in a subtree at most 4 subtrees away from the leaf's own; slots at or beyond far_count are padding. links[d, l, k] is the same for all d in one aligned block of 2^l subtrees.
All inputs are finite; a program needn't handle non-finite values.
Results may differ from a plain program's by a relative error of at most 0.0001.
Values sent between devices are 32-bit elements; how exact they have to be, the bound alone decides.
No kernel may reach another device: no remote copies, remote signals or barrier semaphores. Data moves between devices by JAX's collectives and lax.ppermute only.
A program may use at most 64 MiB of HBM per device.

v0:
```python
import functools

import jax
import jax.numpy as jnp
from jax import lax
from jax.experimental import pallas as pl
from jax.experimental.pallas import tpu as pltpu
from jax.sharding import PartitionSpec as P

REACH = 4
DEPTH = 4
OFFSETS = (-3, -2, 2, 3)
GROUP = 2 * REACH
LANES = 128
TILE = 8
VMEM_LIMIT = 64 * 1024 * 1024

NN = (((1,), (0,)), ((), ()))
NT = (((1,), (1,)), ((), ()))

VMEM = pl.BlockSpec(memory_space=pltpu.VMEM)
SMEM = pl.BlockSpec(memory_space=pltpu.SMEM)
HBM = pl.BlockSpec(memory_space=pltpu.HBM)
PARAMS = pltpu.CompilerParams(vmem_limit_bytes=VMEM_LIMIT)
F32 = jnp.float32
BF16 = jnp.bfloat16


def halves(x):
    high = x.astype(BF16)
    low = (x - high.astype(F32)).astype(BF16)
    return high, low


def dot_halves(a, b_high, b_low, dims):
    a_high, a_low = halves(a)
    rows = a.shape[0]
    both = lax.dot_general(
        jnp.concatenate([a_high, a_low], axis=0), b_high, dims, preferred_element_type=F32
    )
    cross = lax.dot_general(a_high, b_low, dims, preferred_element_type=F32)
    return both[:rows] + (both[rows:] + cross)


def dot3(a, b, dims):
    return dot_halves(a, *halves(b), dims)


def fold(x):
    return jnp.concatenate([x[:TILE], x[TILE:]], axis=1)


def beside(p, q):
    rank = p.shape[1] // 2
    left = lax.broadcasted_iota(jnp.int32, p.shape, 1) < rank
    return jnp.concatenate(
        [
            jnp.where(left, p, pltpu.roll(q, rank, 1)),
            jnp.where(left, pltpu.roll(p, rank, 1), q),
        ],
        axis=0,
    )


def row_of(tiles):
    return jnp.concatenate([beside(*tiles[k : k + 2]) for k in range(0, len(tiles), 2)], axis=1)


def lane_gather(x, high, low):
    rows, columns = x.shape
    high = jnp.broadcast_to(high, (rows, LANES))
    low = jnp.broadcast_to(low, (rows, LANES))
    result = jnp.zeros((rows, LANES), x.dtype)
    for source in range(columns // LANES):
        tile = x[:, source * LANES : (source + 1) * LANES]
        moved = jnp.take_along_axis(tile, low, axis=1, mode="promise_in_bounds")
        result = jnp.where(high == source, moved, result)
    return result


def fetch(pairs, sems):
    copies = [
        pltpu.make_async_copy(source, target, sems.at[index])
        for index, (source, target) in enumerate(pairs)
    ]
    for copy in copies:
        copy.start()
    return copies


def up_kernel(
    me_ref, points_hbm, order_hbm, bases_hbm, lift_hbm, out, x_out, points_v, order_v, bases_v, lift_v, sems
):
    copies = fetch(
        [(order_hbm, order_v), (points_hbm, points_v), (bases_hbm, bases_v), (lift_hbm, lift_v)], sems
    )
    me = me_ref[0]
    leaf_dev, rank, leaf_size = bases_v.shape
    vectors, points_dev = points_v.shape
    copies[0].wait()
    copies[1].wait()
    points = points_v[...]
    per_leaf = leaf_size // LANES
    for t in range(points_dev // LANES):
        spot = order_v[t : t + 1, :] - me * points_dev
        column = t % per_leaf * LANES
        x_out[t // per_leaf, :, column : column + LANES] = lane_gather(
            points, lax.shift_right_logical(spot, 7), spot & (LANES - 1)
        )
    copies[2].wait()
    coefs = [dot3(x_out[leaf], bases_v[leaf], NT) for leaf in range(leaf_dev)]
    tiles = [fold(coef) for coef in coefs]
    copies[3].wait()
    weights = lift_v[...].reshape(leaf_dev * rank, rank)
    tiles.append(fold(dot3(jnp.concatenate(coefs, axis=1), weights, NN)))
    for peer in range(GROUP):
        for index, tile in enumerate(tiles):
            out[peer, index * TILE : (index + 1) * TILE, :] = tile
    place = lax.rem(me, GROUP)
    start = len(tiles) * TILE
    for part in range(per_leaf):
        first = x_out[0, :, part * LANES : (part + 1) * LANES]
        last = x_out[leaf_dev - 1, :, part * LANES : (part + 1) * LANES]
        rows = slice(start + part * vectors, start + (part + 1) * vectors)
        for peer in range(GROUP):
            above = lax.rem(place + 1, GROUP) == peer
            out[peer, rows, :] = jnp.where(above, last, first)


def side_kernel(me_ref, *refs):
    inputs, outputs = refs[:11], refs[11:23]
    held, results = refs[23:34], refs[34:46]
    sems, block_sems, out_sems = refs[46:]
    ids_s, links_s, x_ref, order_v, transfer_v, couple_v, top_v, lift_v, far_v, bases_v, blocks_v = held
    (
        inverse_out,
        up_high,
        up_low,
        path_high,
        path_low,
        leaf_high,
        leaf_low,
        bases_high,
        bases_low,
        near_out,
        edge_high,
        edge_low,
    ) = results
    copies = fetch(list(zip(inputs[:-1], held[:-1])), sems)
    leaf_dev, slots, leaf_size, _ = blocks_v.shape
    blocks = fetch([(inputs[-1].at[leaf], blocks_v.at[leaf]) for leaf in range(leaf_dev)], block_sems)
    writes = [
        pltpu.make_async_copy(source, target, out_sems.at[index])
        for index, (source, target) in enumerate(zip(results, outputs))
    ]
    me = me_ref[0]
    _, rank, _ = bases_v.shape

    for copy in copies[:4]:
        copy.wait()
    points_dev = order_v.shape[1]
    tiles = points_dev // LANES
    spot = order_v[...] - me * points_dev
    times = lax.broadcasted_iota(jnp.int32, (1, points_dev), 1)
    shape = (tiles, points_dev)
    match = lax.broadcasted_iota(jnp.int32, shape, 0) == lax.shift_right_logical(spot, 7)
    digits = [
        jnp.where(match, jnp.broadcast_to(digit.astype(F32), shape), 0.0)
        for digit in (lax.shift_right_logical(times, 4), times & 15)
    ]
    shape = (LANES, points_dev)
    match = lax.broadcasted_iota(jnp.int32, shape, 0) == (spot & (LANES - 1))
    both = lax.dot_general(
        jnp.concatenate(digits, axis=0).astype(BF16),
        jnp.where(match, 1.0, 0.0).astype(BF16),
        NT,
        preferred_element_type=F32,
    )
    inverse_out[...] = (both[:tiles] * 16.0 + both[tiles:]).astype(jnp.int32)
    writes[0].start()

    for copy in copies[4:7]:
        copy.wait()
    composed = transfer_v[0].reshape(2 * rank, rank)
    row = 0
    for level in range(1, DEPTH):
        rows = composed.shape[0]
        up_high[row : row + rows], up_low[row : row + rows] = halves(composed)
        row += rows
        if level < DEPTH - 1:
            composed = jnp.concatenate(
                [dot3(composed, transfer_v[level, side], NN) for side in range(2)], axis=0
            )
    writes[1].start()
    writes[2].start()

    path = None
    for level in range(DEPTH):
        weights = []
        for column in range(len(OFFSETS)):
            link = links_s[level, column].astype(F32)
            weights.append(link * couple_v[level, column])
        weights = jnp.concatenate(weights, axis=1)
        step = transfer_v[level, lax.shift_right_logical(me, level) & 1]
        if path is not None:
            weights = dot3(path, weights, NN)
            step = dot3(path, step, NN)
        path = step
        column = level * len(OFFSETS) * rank
        span = slice(column, column + weights.shape[1])
        path_high[:, span], path_low[:, span] = halves(weights)
    top = dot3(path, top_v[...], NN)
    last = jnp.concatenate(
        [dot3(top, transfer_v[DEPTH - 1, side], NT) for side in range(2)], axis=1
    )
    column = DEPTH * len(OFFSETS) * rank
    span = slice(column, column + 2 * rank)
    path_high[:, span], path_low[:, span] = halves(last)
    writes[3].start()
    writes[4].start()

    for copy in copies[7:]:
        copy.wait()
    for leaf in range(leaf_dev):
        row = [far_v[leaf, slot] for slot in range(far_v.shape[1])] + [lift_v[leaf]]
        leaf_high[leaf], leaf_low[leaf] = halves(jnp.concatenate(row, axis=1))
        bases_high[leaf], bases_low[leaf] = halves(bases_v[leaf])
    for write in writes[5:9]:
        write.start()

    for leaf in range(leaf_dev):
        blocks[leaf].wait()
        total = jnp.zeros(near_out.shape[1:], F32)
        for slot in range(slots):
            local = ids_s[slot, leaf] - me * leaf_dev
            here = (local >= 0) & (local < leaf_dev)
            x_leaf = jnp.where(here, x_ref[jnp.clip(local, 0, leaf_dev - 1)], 0.0)
            total = total + dot3(x_leaf, blocks_v[leaf, slot], NT)
        near_out[leaf] = total

    for index, leaf, outside in ((0, 0, -1), (1, leaf_dev - 1, leaf_dev)):
        total = jnp.zeros((leaf_size, leaf_size), F32)
        for slot in range(1, slots):
            remote = ids_s[slot, leaf] - me * leaf_dev == outside
            total = total + jnp.where(remote, blocks_v[leaf, slot], 0.0)
        edge_high[index], edge_low[index] = halves(total)
    for write in writes[9:]:
        write.start()
    for write in writes:
        write.wait()


def half_kernel(rows, me_ref, group_hbm, side_hbm, out, sems):
    del side_hbm
    low = lax.rem(me_ref[0], GROUP) < REACH
    edge_rows = out.shape[0] - REACH * rows
    first = jnp.where(low, REACH, 0)
    moves = [
        (group_hbm.at[first + part, pl.ds(0, rows)], out.at[pl.ds(part * rows, rows)])
        for part in range(REACH)
    ]
    moves.append(
        (
            group_hbm.at[jnp.where(low, GROUP - 1, 0), pl.ds(rows, edge_rows)],
            out.at[pl.ds(REACH * rows, edge_rows)],
        )
    )
    for copy in fetch(moves, sems):
        copy.wait()


def node_kernel(
    leaf_dev, group_hbm, half_hbm, up_high_hbm, up_low_hbm, out, roots_v, up_high, up_low, sems
):
    del half_hbm
    copies = fetch(
        [
            (group_hbm.at[:, pl.ds(leaf_dev * TILE, TILE), :], roots_v),
            (up_high_hbm, up_high),
            (up_low_hbm, up_low),
        ],
        sems,
    )
    for copy in copies:
        copy.wait()
    roots = [roots_v[peer] for peer in range(GROUP)]
    start, tiles = 0, []
    for level in range(1, DEPTH):
        width = 1 << level
        count = GROUP // width
        left = jnp.concatenate(
            [row_of(roots[n * width : (n + 1) * width]) for n in range(count)], axis=0
        )
        size = left.shape[1]
        nodes = dot_halves(left, up_high[start : start + size], up_low[start : start + size], NN)
        start += size
        tiles += [fold(nodes[n * 2 * TILE : (n + 1) * 2 * TILE]) for n in range(count)]
    tiles.append(jnp.zeros((TILE, LANES), F32))
    for peer in range(out.shape[0]):
        for index, tile in enumerate(tiles):
            out[peer, index] = tile


def down_kernel(me_ref, *refs):
    count = (len(refs) - 3) // 2
    out_ref, y_tree, sems = refs[count], refs[-2], refs[-1]
    held = refs[count + 1 : -2]
    copies = fetch(list(zip(refs[:count], held)), sems)
    (
        group_ref,
        half_ref,
        nodes_ref,
        path_high,
        path_low,
        far_ids_s,
        far_count_s,
        edge_high,
        edge_low,
        leaf_high,
        leaf_low,
        bases_high,
        bases_low,
        near_ref,
        inverse_ref,
    ) = held
    me = me_ref[0]
    leaf_dev, vectors, leaf_size = near_ref.shape
    points_dev = out_ref.shape[1]
    groups = nodes_ref.shape[0]
    slots = far_ids_s.shape[1]
    group = lax.shift_right_logical(me, 3)
    place = me & (GROUP - 1)
    low = place < REACH
    per_leaf = leaf_size // LANES
    start = (leaf_dev + 1) * TILE

    def tile_of(subtree, index):
        other = subtree & (GROUP - 1)
        inside = lax.shift_right_arithmetic(subtree, 3) == group
        row = pl.multiple_of(index * TILE, TILE)
        near_row = jnp.clip(other - jnp.where(low, REACH, 0), 0, REACH - 1) * start
        here = group_ref[other, pl.ds(row, TILE), :]
        there = half_ref[pl.ds(pl.multiple_of(near_row + row, TILE), TILE), :]
        return jnp.where(inside, here, there)

    for copy in copies[:5]:
        copy.wait()
    partners = []
    for level in range(DEPTH):
        node = lax.shift_right_logical(me, level)
        size = (groups * GROUP) >> level
        for offset in OFFSETS:
            other = node + offset
            used = (other >= 0) & (other < size)
            other = jnp.clip(other, 0, size - 1)
            if level == 0:
                tile = tile_of(other, leaf_dev)
            else:
                shift = DEPTH - 1 - level
                first = GROUP - (2 << shift)
                tile = nodes_ref[
                    lax.shift_right_logical(other, shift), first + (other & ((1 << shift) - 1))
                ]
            partners.append(jnp.where(used, tile, 0.0))
    top = lax.shift_right_logical(me, DEPTH)
    for side in range(2):
        blended = jnp.zeros((TILE, LANES), F32)
        for other in range(groups // 2):
            distance = jnp.abs(top - other)
            weight = jnp.where(distance >= 2, 1.0 / jnp.maximum(distance, 1).astype(F32), 0.0)
            blended = blended + weight * nodes_ref[2 * other + side, GROUP - 2]
        partners.append(blended)
    down = dot_halves(row_of(partners), path_high[...], path_low[...], NT)

    for copy in copies[5:9]:
        copy.wait()
    edges = []
    for index, offset in ((0, -1), (1, 1)):
        other = me + offset
        inside = lax.shift_right_arithmetic(other, 3) == group
        here = group_ref[other & (GROUP - 1), start:, :]
        chosen = jnp.where(inside, here, half_ref[REACH * start :, :])
        edges.append(
            jnp.concatenate(
                [chosen[part * vectors : (part + 1) * vectors] for part in range(per_leaf)], axis=1
            )
        )
    edge_parts = [
        dot_halves(edges[index], edge_high[index], edge_low[index], NT) for index in range(2)
    ]

    for copy in copies[9:]:
        copy.wait()
    for leaf in range(leaf_dev):
        picked = []
        for slot in range(slots):
            used = slot < far_count_s[leaf]
            spot = far_ids_s[leaf, slot]
            tile = tile_of(lax.shift_right_logical(spot, 3), spot & (leaf_dev - 1))
            picked.append(jnp.where(used, tile, 0.0))
        left = jnp.concatenate([row_of(picked), down], axis=1)
        leaf_out = dot_halves(left, leaf_high[leaf], leaf_low[leaf], NT)
        y_leaf = near_ref[leaf] + dot_halves(leaf_out, bases_high[leaf], bases_low[leaf], NN)
        if leaf == 0:
            y_leaf = y_leaf + edge_parts[0]
        if leaf == leaf_dev - 1:
            y_leaf = y_leaf + edge_parts[1]
        y_tree[:, leaf * leaf_size : (leaf + 1) * leaf_size] = y_leaf

    y = y_tree[...]
    for tile in range(points_dev // LANES):
        spot = inverse_ref[tile : tile + 1, :]
        out_ref[:, tile * LANES : (tile + 1) * LANES] = lane_gather(
            y, lax.shift_right_logical(spot, 7), spot & (LANES - 1)
        )


def local(
    devices,
    points,
    order,
    bases,
    lift,
    near_ids,
    near_blocks,
    far_ids,
    far_count,
    far_blocks,
    transfer,
    couple,
    links,
    top_couple,
):
    me = lax.axis_index("leaf").astype(jnp.int32).reshape(1)
    vectors, points_dev = points.shape
    leaf_dev, leaf_size, rank = bases.shape
    slots = near_ids.shape[1]
    far_slots = far_ids.shape[1]
    bases_t = jnp.swapaxes(bases, 1, 2)
    tiles = points_dev // LANES
    edge_rows = vectors * (leaf_size // LANES)
    rows = (leaf_dev + 1) * TILE
    groups = devices // GROUP
    order_tiles = order.reshape(tiles, LANES)
    shape = jax.ShapeDtypeStruct

    group_out, tree_x = pl.pallas_call(
        up_kernel,
        out_shape=[
            shape((GROUP, rows + edge_rows, LANES), F32),
            shape((leaf_dev, vectors, leaf_size), F32),
        ],
        in_specs=[SMEM] + [HBM] * 4,
        out_specs=[VMEM] * 2,
        scratch_shapes=[
            pltpu.VMEM(points.shape, F32),
            pltpu.VMEM((tiles, LANES), jnp.int32),
            pltpu.VMEM(bases_t.shape, F32),
            pltpu.VMEM(lift.shape, F32),
            pltpu.SemaphoreType.DMA((4,)),
        ],
        compiler_params=PARAMS,
        name="up",
    )(me, points, order_tiles, bases_t, lift)

    aligned = [[g * GROUP + i for i in range(GROUP)] for g in range(groups)]
    group_in = lax.all_to_all(group_out, "leaf", 0, 0, axis_index_groups=aligned, tiled=True)

    ids_t = near_ids.T
    links_own = links.reshape(links.shape[1:])
    composed_rows = (2 + 4 + 8) * rank
    path_columns = (DEPTH * len(OFFSETS) + 2) * rank
    leaf_columns = (far_slots + 1) * rank
    both = lambda *size: [shape(size, BF16)] * 2
    operands = (
        ids_t,
        links_own,
        tree_x,
        order.reshape(1, points_dev),
        transfer,
        couple,
        top_couple,
        lift,
        far_blocks,
        bases_t,
        near_blocks,
    )
    results = (
        [shape((tiles, LANES), jnp.int32)]
        + both(composed_rows, rank)
        + both(rank, path_columns)
        + both(leaf_dev, rank, leaf_columns)
        + both(leaf_dev, rank, leaf_size)
        + [shape(tree_x.shape, F32)]
        + both(2, leaf_size, leaf_size)
    )
    (
        inverse,
        up_high,
        up_low,
        path_high,
        path_low,
        leaf_high,
        leaf_low,
        bases_high,
        bases_low,
        near_part,
        edge_high,
        edge_low,
    ) = pl.pallas_call(
        side_kernel,
        out_shape=results,
        in_specs=[SMEM] + [HBM] * len(operands),
        out_specs=[HBM] * len(results),
        scratch_shapes=[
            (pltpu.SMEM if x is ids_t or x is links_own else pltpu.VMEM)(x.shape, x.dtype)
            for x in operands
        ]
        + [pltpu.VMEM(x.shape, x.dtype) for x in results]
        + [
            pltpu.SemaphoreType.DMA((len(operands) - 1,)),
            pltpu.SemaphoreType.DMA((leaf_dev,)),
            pltpu.SemaphoreType.DMA((len(results),)),
        ],
        compiler_params=PARAMS,
        cost_estimate=pl.CostEstimate(
            flops=6 * vectors * near_blocks.size,
            bytes_accessed=4 * near_blocks.size,
            transcendentals=0,
        ),
        name="side",
    )(me, *operands)

    half_out = pl.pallas_call(
        functools.partial(half_kernel, rows),
        out_shape=shape((REACH * rows + edge_rows, LANES), F32),
        in_specs=[SMEM, HBM, HBM],
        out_specs=VMEM,
        scratch_shapes=[pltpu.SemaphoreType.DMA((REACH + 1,))],
        compiler_params=PARAMS,
        name="half",
    )(me, group_in, inverse)
    nodes_out = pl.pallas_call(
        functools.partial(node_kernel, leaf_dev),
        out_shape=shape((groups, GROUP, TILE, LANES), F32),
        in_specs=[HBM] * 4,
        out_specs=VMEM,
        scratch_shapes=[
            pltpu.VMEM((GROUP, TILE, LANES), F32),
            pltpu.VMEM(up_high.shape, BF16),
            pltpu.VMEM(up_low.shape, BF16),
            pltpu.SemaphoreType.DMA((3,)),
        ],
        compiler_params=PARAMS,
        name="nodes",
    )(group_in, half_out, up_high, up_low)

    pairs = []
    for device in range(devices):
        target = device + GROUP if device % GROUP < REACH else device - GROUP
        if 0 <= target < devices:
            pairs.append((device, target))
    half_in = lax.ppermute(half_out, "leaf", pairs)
    across = [[g * GROUP + i for g in range(groups)] for i in range(GROUP)]
    nodes_in = lax.all_to_all(nodes_out, "leaf", 0, 0, axis_index_groups=across, tiled=True)

    operands = (
        group_in,
        half_in,
        nodes_in,
        path_high,
        path_low,
        far_ids,
        far_count,
        edge_high,
        edge_low,
        leaf_high,
        leaf_low,
        bases_high,
        bases_low,
        near_part,
        inverse,
    )
    return pl.pallas_call(
        down_kernel,
        out_shape=shape((vectors, points_dev), F32),
        in_specs=[SMEM] + [HBM] * len(operands),
        out_specs=VMEM,
        scratch_shapes=[
            (pltpu.SMEM if x is far_ids or x is far_count else pltpu.VMEM)(x.shape, x.dtype)
            for x in operands
        ]
        + [pltpu.VMEM((vectors, points_dev), F32), pltpu.SemaphoreType.DMA((len(operands),))],
        compiler_params=PARAMS,
        name="down",
    )(me, *operands)


def solution(mesh):
    in_specs = (
        P(None, "leaf"),
        P("leaf"),
        P("leaf", None, None),
        P("leaf", None, None),
        P("leaf", None),
        P("leaf", None, None, None),
        P("leaf", None),
        P("leaf"),
        P("leaf", None, None, None),
        P(),
        P(),
        P("leaf", None, None),
        P(),
    )
    return jax.shard_map(
        functools.partial(local, mesh.shape["leaf"]),
        mesh=mesh,
        in_specs=in_specs,
        out_specs=P(None, "leaf"),
        check_vma=False,
    )
```

profile of v0, /device:TPU:12, one launch (start us, length us, event | category | flops | bytes accessed | tf_op | source)
XLA Modules:
  0.0 39.8 jit_solution(11015466055032265160)
XLA Ops:
  0.0 3.0 %up.1 = (f32[8,104,128]{2,1,0:T(8,128)}, f32[8,16,256]{2,1,0:T(8,128)}) custom-call(s32[1]{0:T(128)} %bitcast.me_ref, f32[16,2048]{1,0:T(8,128)} %points_hbm.1, s32[16,128]{1,0:T(8,128)} %bitcast.8, f32[8,64,256]{2,1,0:T(8,128)} %bitcast.6, f32[8,64,64]{2,1,0:T(8,128)} %refs_7_.1), custom_call_target="tpu_custom_call" | custom-call | tf_op jit(solution)/shard_map/up/pallas_call | solution.py:447
  3.0 4.5 %all-to-all-start = ((f32[8,104,128]{2,1,0:T(8,128)}), f32[8,104,128]{2,1,0:T(8,128)}, u32[]{:S(2)}, u32[]{:S(2)}) async-start(f32[8,104,128]{2,1,0:T(8,128)} %get-tuple-element.19), calls=%async_computation | async-start | bytes 851968 | tf_op jit(solution)/shard_map/all_to_all | solution.py:467
  7.5 9.6 %side.1 = (s32[16,128]{1,0:T(8,128)}, bf16[896,64]{1,0:T(8,128)(2,1)}, bf16[896,64]{1,0:T(8,128)(2,1)}, bf16[64,1152]{1,0:T(8,128)(2,1)}, bf16[64,1152]{1,0:T(8,...) custom-call(s32[1]{0:T(128)} %bitcast.me_ref, ...), custom_call_target="tpu_custom_call" | custom-call | flops 150994944 | bytes 6291456 | tf_op jit(solution)/shard_map/side/pallas_call | solution.py:510
  17.1 0.0 all-to-all-done.group_hbm.refs_0_
  17.1 1.5 %half.1.half_hbm = f32[320,128]{1,0:T(8,128)} custom-call(s32[1]{0:T(128)} %bitcast.me_ref, f32[8,104,128]{2,1,0:T(8,128)} %all-to-all-done.group_hbm.refs_0_, s32[16,128]{1,0:T(8,128)} %get-tuple-element.21.side_hbm.refs_14_), custom_call_target="tpu_custom_call" | custom-call | tf_op jit(solution)/shard_map/half/pallas_call | solution.py:534
  18.7 2.1 %nodes.1 = f32[4,8,8,128]{3,2,1,0:T(8,128)} custom-call(f32[8,104,128]{2,1,0:T(8,128)} %all-to-all-done.group_hbm.refs_0_, f32[320,128]{1,0:T(8,128)} %half.1.half_hbm, bf16[896,64]{1,0:T(8,128)(2,1)} %get-tuple-element.22.up_high_hbm, bf16[896,64]{1,0:T(8,128)(2,1)} %get-tuple-element.23.up_low_hbm), custom_call_target="tpu_custom_call" | custom-call | tf_op jit(solution)/shard_map/nodes/pallas_call | solution.py:543
  20.8 5.3 %all-to-all-start.1 = ((f32[4,8,8,128]{3,2,1,0:T(8,128)}), f32[4,8,8,128]{3,2,1,0:T(8,128)}, u32[]{:S(2)}, u32[]{:S(2)}) async-start(f32[4,8,8,128]{3,2,1,0:T(8,128)} %nodes.1), calls=%async_computation.1 | async-start | bytes 262144 | tf_op jit(solution)/shard_map/all_to_all | solution.py:565
  26.1 1.9 %collective-permute-start = (f32[320,128]{1,0:T(8,128)}, f32[320,128]{1,0:T(8,128)}, u32[]{:S(2)}, u32[]{:S(2)}) collective-permute-start(f32[320,128]{1,0:T(8,128)} %half.1.half_hbm), channel_id=1, source_target_pairs={{0,8},{1,9},{2,10},{3,11},{8,16},{9,17},{10,18},{11,19},{12,4},{13... | collective-permute-start | bytes 491528 | tf_op jit(solution)/shard_map/ppermute | solution.py:563
  28.0 6.8 %collective-permute-done.refs_1_ = f32[320,128]{1,0:T(8,128)} collective-permute-done((f32[320,128]{1,0:T(8,128)}, f32[320,128]{1,0:T(8,128)}, u32[]{:S(2)}, u32[]{:S(2)}) %collective-permute-start) | collective-permute-done | bytes 163872 | tf_op jit(solution)/shard_map/ppermute | solution.py:563
  34.8 0.0 all-to-all-done.1.refs_2_
  34.8 4.9 %down.1 = f32[16,2048]{1,0:T(8,128)} custom-call(s32[1]{0:T(128)} %bitcast.me_ref, f32[8,104,128]{2,1,0:T(8,128)} %all-to-all-done.group_hbm.refs_0_, f32[320,128]{1,0:T(8,128)} %collective-permute-done.refs_1_, f32[4,8,8,128]{3,2,1,0:T(8,128)} %all-to-all-done.1.refs_2_, bf16[64,1152]{1,0:T(8,128)(2,1)} %get-tuple-element.24.refs_3_, ...), custom_call_target="tpu_custom_call" | custom-call | tf_op jit(solution)/shard_map/down/pallas_call | solution.py:584
Async XLA Ops:
  3.0 14.1 %all-to-all-start = ((f32[8,104,128]{2,1,0:T(8,128)}), f32[8,104,128]{2,1,0:T(8,128)}, u32[]{:S(2)}, u32[]{:S(2)}) async-start(f32[8,104,128]{2,1,0:T(8,128)} %get-tuple-element.19), calls=%async_computation | async-start | bytes 851968 | tf_op jit(solution)/shard_map/all_to_all | solution.py:467
  20.8 14.1 %all-to-all-start.1 = ((f32[4,8,8,128]{3,2,1,0:T(8,128)}), f32[4,8,8,128]{3,2,1,0:T(8,128)}, u32[]{:S(2)}, u32[]{:S(2)}) async-start(f32[4,8,8,128]{3,2,1,0:T(8,128)} %nodes.1), calls=%async_computation.1 | async-start | bytes 262144 | tf_op jit(solution)/shard_map/all_to_all | solution.py:565
  26.1 8.7 %collective-permute-start = (f32[320,128]{1,0:T(8,128)}, f32[320,128]{1,0:T(8,128)}, u32[]{:S(2)}, u32[]{:S(2)}) collective-permute-start(f32[320,128]{1,0:T(8,128)} %half.1.half_hbm), channel_id=1, source_target_pairs={{0,8},{1,9},{2,10},{3,11},{8,16},{9,17},{10,18},{11,19},{12,4},{13... | collective-permute-start | bytes 491528 | tf_op jit(solution)/shard_map/ppermute | solution.py:563
where the time goes:
time: 40.2 us; the launch traced here: 39.8 us
  Pallas kernels  21.1 us (52%)
  starting transfers between devices  11.8 us (29%)
  waiting for transfers between devices  6.82 us (17%)
    pallas_call x1, Pallas kernels, local(): pl.pallas_call(side_kernel, out_shape=results, in_specs=[SMEM] + [HBM] *...  9.59 us
    ppermute x1, waiting for transfers between devices, local(): half_in = lax.ppermute(half_out, 'leaf', pairs)  6.81 us
    all_to_all x1, starting transfers between devices, local(): lax.all_to_all(nodes_out, 'leaf', 0, 0, axis_index_groups=across, tiled=T...  5.33 us
    pallas_call x1, Pallas kernels, local(): pl.pallas_call(down_kernel, out_shape=shape((vectors, points_dev), F32),...  4.91 us
    all_to_all x1, starting transfers between devices, local(): lax.all_to_all(group_out, 'leaf', 0, 0, axis_index_groups=aligned, tiled=...  4.53 us
    pallas_call x1, Pallas kernels, local(): pl.pallas_call(up_kernel, out_shape=[shape((GROUP, rows + edge_rows, LANE...  2.99 us
    pallas_call x1, Pallas kernels, local(): pl.pallas_call(functools.partial(node_kernel, leaf_dev), out_shape=shape(...  2.07 us
    ppermute x1, starting transfers between devices, local(): half_in = lax.ppermute(half_out, 'leaf', pairs)  1.91 us
  transfers between devices with their start and end apart: 3, of which 1 were waited for; matrix products, arithmetic and copies ran while one was open for 0% of the time, Pallas kernels for 24%

commit v1 on v0

--- a/solution.py
+++ b/solution.py
@@ -13,6 +13,7 @@
 GROUP = 2 * REACH
 LANES = 128
 TILE = 8
+NODES = GROUP - 1
 VMEM_LIMIT = 64 * 1024 * 1024
 
 NN = (((1,), (0,)), ((), ()))
@@ -130,106 +131,118 @@
 def side_kernel(me_ref, *refs):
     inputs, outputs = refs[:11], refs[11:23]
     held, results = refs[23:34], refs[34:46]
-    sems, block_sems, out_sems = refs[46:]
-    ids_s, links_s, x_ref, order_v, transfer_v, couple_v, top_v, lift_v, far_v, bases_v, blocks_v = held
+    sems, leaf_sems, out_sems, leaf_out_sems = refs[46:]
+    ids_s, links_s, transfer_v, couple_v, x_ref, top_v, lift_v, order_v, far_v, bases_v, blocks_v = held
     (
         inverse_out,
         up_high,
         up_low,
         path_high,
         path_low,
+        near_out,
+        edge_high,
+        edge_low,
         leaf_high,
         leaf_low,
         bases_high,
         bases_low,
-        near_out,
-        edge_high,
-        edge_low,
     ) = results
-    copies = fetch(list(zip(inputs[:-1], held[:-1])), sems)
     leaf_dev, slots, leaf_size, _ = blocks_v.shape
-    blocks = fetch([(inputs[-1].at[leaf], blocks_v.at[leaf]) for leaf in range(leaf_dev)], block_sems)
-    writes = [
-        pltpu.make_async_copy(source, target, out_sems.at[index])
-        for index, (source, target) in enumerate(zip(results, outputs))
+    _, rank, _ = bases_v.shape
+    copies = fetch(list(zip(inputs[:8], held[:8])), sems)
+    by_leaf = [
+        fetch([(x.at[leaf], v.at[leaf]) for x, v in zip(inputs[8:], held[8:])], leaf_sems.at[leaf])
+        for leaf in range(leaf_dev)
     ]
+    writes = []
+
+    def write(*indices):
+        for index in indices:
+            writes.extend(
+                fetch([(results[index], outputs[index])], out_sems.at[pl.ds(index, 1)])
+            )
+
     me = me_ref[0]
-    _, rank, _ = bases_v.shape
-
-    for copy in copies[:4]:
-        copy.wait()
-    points_dev = order_v.shape[1]
-    tiles = points_dev // LANES
-    spot = order_v[...] - me * points_dev
-    times = lax.broadcasted_iota(jnp.int32, (1, points_dev), 1)
-    shape = (tiles, points_dev)
-    match = lax.broadcasted_iota(jnp.int32, shape, 0) == lax.shift_right_logical(spot, 7)
-    digits = [
-        jnp.where(match, jnp.broadcast_to(digit.astype(F32), shape), 0.0)
-        for digit in (lax.shift_right_logical(times, 4), times & 15)
-    ]
-    shape = (LANES, points_dev)
-    match = lax.broadcasted_iota(jnp.int32, shape, 0) == (spot & (LANES - 1))
-    both = lax.dot_general(
-        jnp.concatenate(digits, axis=0).astype(BF16),
-        jnp.where(match, 1.0, 0.0).astype(BF16),
-        NT,
-        preferred_element_type=F32,
-    )
-    inverse_out[...] = (both[:tiles] * 16.0 + both[tiles:]).astype(jnp.int32)
-    writes[0].start()
-
-    for copy in copies[4:7]:
-        copy.wait()
-    composed = transfer_v[0].reshape(2 * rank, rank)
-    row = 0
-    for level in range(1, DEPTH):
-        rows = composed.shape[0]
-        up_high[row : row + rows], up_low[row : row + rows] = halves(composed)
-        row += rows
-        if level < DEPTH - 1:
-            composed = jnp.concatenate(
-                [dot3(composed, transfer_v[level, side], NN) for side in range(2)], axis=0
-            )
-    writes[1].start()
-    writes[2].start()
-
-    path = None
-    for level in range(DEPTH):
-        weights = []
-        for column in range(len(OFFSETS)):
-            link = links_s[level, column].astype(F32)
-            weights.append(link * couple_v[level, column])
-        weights = jnp.concatenate(weights, axis=1)
-        step = transfer_v[level, lax.shift_right_logical(me, level) & 1]
-        if path is not None:
-            weights = dot3(path, weights, NN)
-            step = dot3(path, step, NN)
-        path = step
-        column = level * len(OFFSETS) * rank
-        span = slice(column, column + weights.shape[1])
+    bits = [lax.shift_right_logical(me, level) & 1 for level in range(DEPTH)]
+
+    def put_up(row, weights):
+        span = slice(row, row + weights.shape[0])
+        up_high[span], up_low[span] = halves(weights)
+
+    def put_path(column, weights):
+        span = slice(column * rank, column * rank + weights.shape[1])
         path_high[:, span], path_low[:, span] = halves(weights)
-    top = dot3(path, top_v[...], NN)
-    last = jnp.concatenate(
-        [dot3(top, transfer_v[DEPTH - 1, side], NT) for side in range(2)], axis=1
-    )
-    column = DEPTH * len(OFFSETS) * rank
-    span = slice(column, column + 2 * rank)
-    path_high[:, span], path_low[:, span] = halves(last)
-    writes[3].start()
-    writes[4].start()
-
-    for copy in copies[7:]:
+
+    def couplings(level):
+        return jnp.concatenate(
+            [
+                links_s[level, column].astype(F32) * couple_v[level, column]
+                for column in range(len(OFFSETS))
+            ],
+            axis=1,
+        )
+
+    def inverse():
+        points_dev = order_v.shape[1]
+        tiles = points_dev // LANES
+        spot = order_v[...] - me * points_dev
+        times = lax.broadcasted_iota(jnp.int32, (1, points_dev), 1)
+        shape = (tiles, points_dev)
+        match = lax.broadcasted_iota(jnp.int32, shape, 0) == lax.shift_right_logical(spot, 7)
+        digits = [
+            jnp.where(match, jnp.broadcast_to(digit.astype(F32), shape), 0.0)
+            for digit in (lax.shift_right_logical(times, 4), times & 15)
+        ]
+        shape = (LANES, points_dev)
+        match = lax.broadcasted_iota(jnp.int32, shape, 0) == (spot & (LANES - 1))
+        both = lax.dot_general(
+            jnp.concatenate(digits, axis=0).astype(BF16),
+            jnp.where(match, 1.0, 0.0).astype(BF16),
+            NT,
+            preferred_element_type=F32,
+        )
+        inverse_out[...] = (both[:tiles] * 16.0 + both[tiles:]).astype(jnp.int32)
+
+    def edge(index, leaf, outside):
+        total = jnp.zeros((leaf_size, leaf_size), F32)
+        for slot in range(1, slots):
+            remote = ids_s[slot, leaf] - me * leaf_dev == outside
+            total = total + jnp.where(remote, blocks_v[leaf, slot], 0.0)
+        edge_high[index], edge_low[index] = halves(total)
+
+    def chain():
+        up = transfer_v[0].reshape(2 * rank, rank)
+        path = transfer_v[0, bits[0]]
+        put_up(0, up)
+        put_path(0, couplings(0))
+        row = up.shape[0]
+        for level in range(1, DEPTH):
+            yield
+            if level < DEPTH - 1:
+                up = jnp.concatenate(
+                    [dot3(up, transfer_v[level, side], NN) for side in range(2)], axis=0
+                )
+                put_up(row, up)
+                row += up.shape[0]
+            put_path(level * len(OFFSETS), dot3(path, couplings(level), NN))
+            path = dot3(path, transfer_v[level, bits[level]], NN)
+        write(1, 2)
+        yield
+        top = dot3(path, top_v[...], NN)
+        yield
+        last = [dot3(top, transfer_v[DEPTH - 1, side], NT) for side in range(2)]
+        put_path(DEPTH * len(OFFSETS), jnp.concatenate(last, axis=1))
+        write(3, 4)
+        yield
+        inverse()
+        write(0)
+
+    links = chain()
+    for copy in copies:
         copy.wait()
     for leaf in range(leaf_dev):
-        row = [far_v[leaf, slot] for slot in range(far_v.shape[1])] + [lift_v[leaf]]
-        leaf_high[leaf], leaf_low[leaf] = halves(jnp.concatenate(row, axis=1))
-        bases_high[leaf], bases_low[leaf] = halves(bases_v[leaf])
-    for write in writes[5:9]:
-        write.start()
-
-    for leaf in range(leaf_dev):
-        blocks[leaf].wait()
+        for copy in by_leaf[leaf]:
+            copy.wait()
         total = jnp.zeros(near_out.shape[1:], F32)
         for slot in range(slots):
             local = ids_s[slot, leaf] - me * leaf_dev
@@ -237,50 +250,62 @@
             x_leaf = jnp.where(here, x_ref[jnp.clip(local, 0, leaf_dev - 1)], 0.0)
             total = total + dot3(x_leaf, blocks_v[leaf, slot], NT)
         near_out[leaf] = total
-
-    for index, leaf, outside in ((0, 0, -1), (1, leaf_dev - 1, leaf_dev)):
-        total = jnp.zeros((leaf_size, leaf_size), F32)
-        for slot in range(1, slots):
-            remote = ids_s[slot, leaf] - me * leaf_dev == outside
-            total = total + jnp.where(remote, blocks_v[leaf, slot], 0.0)
-        edge_high[index], edge_low[index] = halves(total)
-    for write in writes[9:]:
-        write.start()
-    for write in writes:
-        write.wait()
-
-
-def half_kernel(rows, me_ref, group_hbm, side_hbm, out, sems):
-    del side_hbm
+        row = [far_v[leaf, slot] for slot in range(far_v.shape[1])] + [lift_v[leaf]]
+        leaf_high[leaf], leaf_low[leaf] = halves(jnp.concatenate(row, axis=1))
+        bases_high[leaf], bases_low[leaf] = halves(bases_v[leaf])
+        if leaf == 0:
+            edge(0, leaf, -1)
+        if leaf == leaf_dev - 1:
+            edge(1, leaf, leaf_dev)
+        next(links, None)
+        writes += fetch(
+            [(v.at[leaf], x.at[leaf]) for v, x in zip(results[8:], outputs[8:])],
+            leaf_out_sems.at[leaf],
+        )
+    for _ in links:
+        pass
+    write(5, 6, 7)
+    for copy in writes:
+        copy.wait()
+
+
+def middle_kernel(
+    leaf_dev,
+    me_ref,
+    group_hbm,
+    up_high_hbm,
+    up_low_hbm,
+    half_out,
+    nodes_out,
+    roots_v,
+    up_high,
+    up_low,
+    sems,
+    half_sems,
+):
     low = lax.rem(me_ref[0], GROUP) < REACH
-    edge_rows = out.shape[0] - REACH * rows
+    copies = fetch(
+        [
+            (group_hbm.at[:, pl.ds(leaf_dev * TILE, TILE), :], roots_v),
+            (up_high_hbm, up_high),
+            (up_low_hbm, up_low),
+        ],
+        sems,
+    )
+    rows = (leaf_dev + 1) * TILE
+    edge_rows = group_hbm.shape[1] - rows
     first = jnp.where(low, REACH, 0)
     moves = [
-        (group_hbm.at[first + part, pl.ds(0, rows)], out.at[pl.ds(part * rows, rows)])
+        (group_hbm.at[first + part, pl.ds(0, rows)], half_out.at[pl.ds(part * rows, rows)])
         for part in range(REACH)
     ]
     moves.append(
         (
             group_hbm.at[jnp.where(low, GROUP - 1, 0), pl.ds(rows, edge_rows)],
-            out.at[pl.ds(REACH * rows, edge_rows)],
-        )
-    )
-    for copy in fetch(moves, sems):
-        copy.wait()
-
-
-def node_kernel(
-    leaf_dev, group_hbm, half_hbm, up_high_hbm, up_low_hbm, out, roots_v, up_high, up_low, sems
-):
-    del half_hbm
-    copies = fetch(
-        [
-            (group_hbm.at[:, pl.ds(leaf_dev * TILE, TILE), :], roots_v),
-            (up_high_hbm, up_high),
-            (up_low_hbm, up_low),
-        ],
-        sems,
-    )
+            half_out.at[pl.ds(REACH * rows, edge_rows)],
+        )
+    )
+    moves = fetch(moves, half_sems)
     for copy in copies:
         copy.wait()
     roots = [roots_v[peer] for peer in range(GROUP)]
@@ -295,21 +320,50 @@
         nodes = dot_halves(left, up_high[start : start + size], up_low[start : start + size], NN)
         start += size
         tiles += [fold(nodes[n * 2 * TILE : (n + 1) * 2 * TILE]) for n in range(count)]
-    tiles.append(jnp.zeros((TILE, LANES), F32))
-    for peer in range(out.shape[0]):
-        for index, tile in enumerate(tiles):
-            out[peer, index] = tile
-
-
-def down_kernel(me_ref, *refs):
-    count = (len(refs) - 3) // 2
-    out_ref, y_tree, sems = refs[count], refs[-2], refs[-1]
-    held = refs[count + 1 : -2]
+    row = REACH * rows + edge_rows
+    for index, tile in enumerate(tiles):
+        half_out[row + index * TILE : row + (index + 1) * TILE, :] = tile
+        for peer in range(nodes_out.shape[0]):
+            nodes_out[peer, index] = tile
+    for copy in moves:
+        copy.wait()
+
+
+def down_kernel(parts, me_ref, *refs):
+    node_parts, refs = refs[:parts], refs[parts:]
+    count = (len(refs) - 5) // 2
+    out_ref = refs[count]
+    held = refs[count + 1 : 2 * count + 1]
+    nodes_ref, y_tree, sems, node_sems = refs[2 * count + 1 :]
+    me = me_ref[0]
+    groups = nodes_ref.shape[0]
+    group = lax.shift_right_logical(me, 3)
+    place = me & (GROUP - 1)
+    low = place < REACH
+    half_hbm = refs[1]
+    if parts > 1:
+        near_by, far_by = jnp.where(low, groups - 1, 1), jnp.where(low, 1, groups - 1)
+        start = half_hbm.shape[0] - NODES * TILE
+        node_copies = fetch(
+            [
+                (part.at[0], nodes_ref.at[lax.rem(group + by, groups)])
+                for part, by in zip(node_parts, (0, far_by, 2))
+            ]
+            + [
+                (
+                    half_hbm.at[pl.ds(start + index * TILE, TILE)],
+                    nodes_ref.at[lax.rem(group + near_by, groups), index],
+                )
+                for index in range(NODES)
+            ],
+            node_sems,
+        )
+    else:
+        node_copies = fetch([(node_parts[0], nodes_ref)], node_sems)
     copies = fetch(list(zip(refs[:count], held)), sems)
     (
         group_ref,
         half_ref,
-        nodes_ref,
         path_high,
         path_low,
         far_ids_s,
@@ -323,16 +377,12 @@
         near_ref,
         inverse_ref,
     ) = held
-    me = me_ref[0]
     leaf_dev, vectors, leaf_size = near_ref.shape
     points_dev = out_ref.shape[1]
-    groups = nodes_ref.shape[0]
     slots = far_ids_s.shape[1]
-    group = lax.shift_right_logical(me, 3)
-    place = me & (GROUP - 1)
-    low = place < REACH
     per_leaf = leaf_size // LANES
     start = (leaf_dev + 1) * TILE
+    edge_rows = group_ref.shape[1] - start
 
     def tile_of(subtree, index):
         other = subtree & (GROUP - 1)
@@ -343,7 +393,7 @@
         there = half_ref[pl.ds(pl.multiple_of(near_row + row, TILE), TILE), :]
         return jnp.where(inside, here, there)
 
-    for copy in copies[:5]:
+    for copy in node_copies + copies[:4]:
         copy.wait()
     partners = []
     for level in range(DEPTH):
@@ -372,14 +422,14 @@
         partners.append(blended)
     down = dot_halves(row_of(partners), path_high[...], path_low[...], NT)
 
-    for copy in copies[5:9]:
+    for copy in copies[4:8]:
         copy.wait()
     edges = []
     for index, offset in ((0, -1), (1, 1)):
         other = me + offset
         inside = lax.shift_right_arithmetic(other, 3) == group
         here = group_ref[other & (GROUP - 1), start:, :]
-        chosen = jnp.where(inside, here, half_ref[REACH * start :, :])
+        chosen = jnp.where(inside, here, half_ref[REACH * start : REACH * start + edge_rows, :])
         edges.append(
             jnp.concatenate(
                 [chosen[part * vectors : (part + 1) * vectors] for part in range(per_leaf)], axis=1
@@ -389,7 +439,7 @@
         dot_halves(edges[index], edge_high[index], edge_low[index], NT) for index in range(2)
     ]
 
-    for copy in copies[9:]:
+    for copy in copies[8:]:
         copy.wait()
     for leaf in range(leaf_dev):
         picked = []
@@ -475,12 +525,12 @@
     operands = (
         ids_t,
         links_own,
-        tree_x,
-        order.reshape(1, points_dev),
         transfer,
         couple,
+        tree_x,
         top_couple,
         lift,
+        order.reshape(1, points_dev),
         far_blocks,
         bases_t,
         near_blocks,
@@ -489,10 +539,10 @@
         [shape((tiles, LANES), jnp.int32)]
         + both(composed_rows, rank)
         + both(rank, path_columns)
+        + [shape(tree_x.shape, F32)]
+        + both(2, leaf_size, leaf_size)
         + both(leaf_dev, rank, leaf_columns)
         + both(leaf_dev, rank, leaf_size)
-        + [shape(tree_x.shape, F32)]
-        + both(2, leaf_size, leaf_size)
     )
     (
         inverse,
@@ -500,13 +550,13 @@
         up_low,
         path_high,
         path_low,
+        near_part,
+        edge_high,
+        edge_low,
         leaf_high,
         leaf_low,
         bases_high,
         bases_low,
-        near_part,
-        edge_high,
-        edge_low,
     ) = pl.pallas_call(
         side_kernel,
         out_shape=results,
@@ -518,9 +568,10 @@
         ]
         + [pltpu.VMEM(x.shape, x.dtype) for x in results]
         + [
-            pltpu.SemaphoreType.DMA((len(operands) - 1,)),
-            pltpu.SemaphoreType.DMA((leaf_dev,)),
-            pltpu.SemaphoreType.DMA((len(results),)),
+            pltpu.SemaphoreType.DMA((8,)),
+            pltpu.SemaphoreType.DMA((leaf_dev, 3)),
+            pltpu.SemaphoreType.DMA((8,)),
+            pltpu.SemaphoreType.DMA((leaf_dev, 4)),
         ],
         compiler_params=PARAMS,
         cost_estimate=pl.CostEstimate(
@@ -531,43 +582,43 @@
         name="side",
     )(me, *operands)
 
-    half_out = pl.pallas_call(
-        functools.partial(half_kernel, rows),
-        out_shape=shape((REACH * rows + edge_rows, LANES), F32),
-        in_specs=[SMEM, HBM, HBM],
-        out_specs=VMEM,
-        scratch_shapes=[pltpu.SemaphoreType.DMA((REACH + 1,))],
-        compiler_params=PARAMS,
-        name="half",
-    )(me, group_in, inverse)
-    nodes_out = pl.pallas_call(
-        functools.partial(node_kernel, leaf_dev),
-        out_shape=shape((groups, GROUP, TILE, LANES), F32),
-        in_specs=[HBM] * 4,
-        out_specs=VMEM,
+    by_permute = groups == 4
+    half_out, nodes_out = pl.pallas_call(
+        functools.partial(middle_kernel, leaf_dev),
+        out_shape=[
+            shape((REACH * rows + edge_rows + NODES * TILE, LANES), F32),
+            shape((1 if by_permute else groups, NODES, TILE, LANES), F32),
+        ],
+        in_specs=[SMEM] + [HBM] * 3,
+        out_specs=[VMEM] * 2,
         scratch_shapes=[
             pltpu.VMEM((GROUP, TILE, LANES), F32),
             pltpu.VMEM(up_high.shape, BF16),
             pltpu.VMEM(up_low.shape, BF16),
             pltpu.SemaphoreType.DMA((3,)),
+            pltpu.SemaphoreType.DMA((REACH + 1,)),
         ],
         compiler_params=PARAMS,
-        name="nodes",
-    )(group_in, half_out, up_high, up_low)
-
-    pairs = []
-    for device in range(devices):
-        target = device + GROUP if device % GROUP < REACH else device - GROUP
-        if 0 <= target < devices:
-            pairs.append((device, target))
-    half_in = lax.ppermute(half_out, "leaf", pairs)
-    across = [[g * GROUP + i for g in range(groups)] for i in range(GROUP)]
-    nodes_in = lax.all_to_all(nodes_out, "leaf", 0, 0, axis_index_groups=across, tiled=True)
+        name="middle",
+    )(me, group_in, up_high, up_low)
+
+    def shifted(x, low, high):
+        pairs = []
+        for device in range(devices):
+            by = low if device % GROUP < REACH else high
+            pairs.append(((device + by * GROUP) % devices, device))
+        return lax.ppermute(x, "leaf", pairs)
+
+    half_in = shifted(half_out, -1, 1)
+    if by_permute:
+        node_parts = (nodes_out, shifted(nodes_out, 1, -1), shifted(nodes_out, 2, 2))
+    else:
+        across = [[g * GROUP + i for g in range(groups)] for i in range(GROUP)]
+        node_parts = (lax.all_to_all(nodes_out, "leaf", 0, 0, axis_index_groups=across, tiled=True),)
 
     operands = (
         group_in,
         half_in,
-        nodes_in,
         path_high,
         path_low,
         far_ids,
@@ -582,18 +633,23 @@
         inverse,
     )
     return pl.pallas_call(
-        down_kernel,
+        functools.partial(down_kernel, len(node_parts)),
         out_shape=shape((vectors, points_dev), F32),
-        in_specs=[SMEM] + [HBM] * len(operands),
+        in_specs=[SMEM] + [HBM] * (len(node_parts) + len(operands)),
         out_specs=VMEM,
         scratch_shapes=[
             (pltpu.SMEM if x is far_ids or x is far_count else pltpu.VMEM)(x.shape, x.dtype)
             for x in operands
         ]
-        + [pltpu.VMEM((vectors, points_dev), F32), pltpu.SemaphoreType.DMA((len(operands),))],
+        + [
+            pltpu.VMEM((groups, NODES, TILE, LANES), F32),
+            pltpu.VMEM((vectors, points_dev), F32),
+            pltpu.SemaphoreType.DMA((len(operands),)),
+            pltpu.SemaphoreType.DMA((len(node_parts) + NODES,)),
+        ],
         compiler_params=PARAMS,
         name="down",
-    )(me, *operands)
+    )(me, *node_parts, *operands)
 
 
 def solution(mesh):

time: 40.2 us -> 36.4 us (0.905)
  the two profiles are of different devices: /device:TPU:12 before, /device:TPU:0 now
where the time goes in v1:
time: 36.4 us; the launch traced here: 36.2 us
  Pallas kernels  19.9 us (55%)
  starting transfers between devices  11.2 us (31%)
  waiting for transfers between devices  5.1 us (14%)
    pallas_call x1, Pallas kernels, local(): pl.pallas_call(side_kernel, out_shape=results, in_specs=[SMEM] + [HBM] *...  9.29 us
    ppermute x3, starting transfers between devices, shifted(): return lax.ppermute(x, 'leaf', pairs)  5.98 us
    pallas_call x1, Pallas kernels, local(): pl.pallas_call(functools.partial(down_kernel, len(node_parts)), out_shape...  5.32 us
    all_to_all x1, starting transfers between devices, local(): lax.all_to_all(group_out, 'leaf', 0, 0, axis_index_groups=aligned, tiled=...  5.19 us
    ppermute x3, waiting for transfers between devices, shifted(): return lax.ppermute(x, 'leaf', pairs)  5.09 us
    pallas_call x1, Pallas kernels, local(): pl.pallas_call(up_kernel, out_shape=[shape((GROUP, rows + edge_rows, LANE...  2.99 us
    pallas_call x1, Pallas kernels, local(): pl.pallas_call(functools.partial(middle_kernel, leaf_dev), out_shape=[sha...  2.27 us
  transfers between devices with their start and end apart: 4, of which 1 were waited for; matrix products, arithmetic and copies ran while one was open for 0% of the time, Pallas kernels for 26%

profile of v1, /device:TPU:0, one launch (start us, length us, event | category | flops | bytes accessed | tf_op | source)
XLA Modules:
  0.0 36.2 jit_solution(1951427992474393377)
XLA Ops:
  0.0 3.0 %up.1 = (f32[8,104,128]{2,1,0:T(8,128)}, f32[8,16,256]{2,1,0:T(8,128)}) custom-call(s32[1]{0:T(128)} %bitcast.me_ref, f32[16,2048]{1,0:T(8,128)} %points_hbm.1, s32[16,128]{1,0:T(8,128)} %bitcast.8, f32[8,64,256]{2,1,0:T(8,128)} %bitcast.6, f32[8,64,64]{2,1,0:T(8,128)} %refs_6_.1), custom_call_target="tpu_custom_call" | custom-call | tf_op jit(solution)/shard_map/up/pallas_call | solution.py:497
  3.0 5.2 %all-to-all-start = ((f32[8,104,128]{2,1,0:T(8,128)}), f32[8,104,128]{2,1,0:T(8,128)}, u32[]{:S(2)}, u32[]{:S(2)}) async-start(f32[8,104,128]{2,1,0:T(8,128)} %get-tuple-element.21), calls=%async_computation | async-start | bytes 851968 | tf_op jit(solution)/shard_map/all_to_all | solution.py:517
  8.2 9.3 %side.1 = (s32[16,128]{1,0:T(8,128)}, bf16[896,64]{1,0:T(8,128)(2,1)}, bf16[896,64]{1,0:T(8,128)(2,1)}, bf16[64,1152]{1,0:T(8,128)(2,1)}, bf16[64,1152]{1,0:T(8,...) custom-call(s32[1]{0:T(128)} %bitcast.me_ref, ...), custom_call_target="tpu_custom_call" | custom-call | flops 150994944 | bytes 6291456 | tf_op jit(solution)/shard_map/side/pallas_call | solution.py:560
  17.5 0.0 all-to-all-done.group_hbm.refs_3_
  17.5 2.3 %middle.1 = (f32[376,128]{1,0:T(8,128)}, f32[1,7,8,128]{3,2,1,0:T(8,128)}) custom-call(s32[1]{0:T(128)} %bitcast.me_ref, f32[8,104,128]{2,1,0:T(8,128)} %all-to-all-done.group_hbm.refs_3_, bf16[896,64]{1,0:T(8,128)(2,1)} %get-tuple-element.23.up_high_hbm, bf16[896,64]{1,0:T(8,128)(2,1)} %get-tuple-element.24.up_low_hbm), custom_call_target="tpu_custom_call" | custom-call | tf_op jit(solution)/shard_map/middle/pallas_call | solution.py:586
  19.8 2.0 %collective-permute-start.2 = (f32[376,128]{1,0:T(8,128)}, f32[376,128]{1,0:T(8,128)}, u32[]{:S(2)}, u32[]{:S(2)}) collective-permute-start(f32[376,128]{1,0:T(8,128)} %get-tuple-element.26), channel_id=1, source_target_pairs={{24,0},{25,1},{26,2},{27,3},{12,4},{13,5},{14,6},{15,7},{0,8},{1,9... | collective-permute-start | bytes 577544 | tf_op jit(solution)/shard_map/ppermute | solution.py:610
  21.8 2.6 %collective-permute-start.1 = (f32[1,7,8,128]{3,2,1,0:T(8,128)}, f32[1,7,8,128]{3,2,1,0:T(8,128)}, u32[]{:S(2)}, u32[]{:S(2)}) collective-permute-start(f32[1,7,8,128]{3,2,1,0:T(8,128)} %get-tuple-element.25.refs_0_), channel_id=1, source_target_pairs={{16,0},{17,1},{18,2},{19,3},{20,4},{21,5},{22,6},{23,7},{24,8},{25... | collective-permute-start | bytes 86024 | tf_op jit(solution)/shard_map/ppermute | solution.py:610
  24.4 1.3 %collective-permute-start = (f32[1,7,8,128]{3,2,1,0:T(8,128)}, f32[1,7,8,128]{3,2,1,0:T(8,128)}, u32[]{:S(2)}, u32[]{:S(2)}) collective-permute-start(f32[1,7,8,128]{3,2,1,0:T(8,128)} %get-tuple-element.25.refs_0_), channel_id=1, source_target_pairs={{8,0},{9,1},{10,2},{11,3},{28,4},{29,5},{30,6},{31,7},{16,8},{17,9... | collective-permute-start | bytes 86024 | tf_op jit(solution)/shard_map/ppermute | solution.py:610
  25.7 5.1 %collective-permute-done.1.refs_2_ = f32[1,7,8,128]{3,2,1,0:T(8,128)} collective-permute-done((f32[1,7,8,128]{3,2,1,0:T(8,128)}, f32[1,7,8,128]{3,2,1,0:T(8,128)}, u32[]{:S(2)}, u32[]{:S(2)}) %collective-permute-start.1) | collective-permute-done | bytes 28704 | tf_op jit(solution)/shard_map/ppermute | solution.py:610
  30.8 0.0 collective-permute-done.refs_1_
  30.8 0.0 collective-permute-done.2.refs_4_
  30.8 5.3 %down.1 = f32[16,2048]{1,0:T(8,128)} custom-call(s32[1]{0:T(128)} %bitcast.me_ref, f32[1,7,8,128]{3,2,1,0:T(8,128)} %get-tuple-element.25.refs_0_, f32[1,7,8,128]{3,2,1,0:T(8,128)} %collective-permute-done.refs_1_, f32[1,7,8,128]{3,2,1,0:T(8,128)} %collective-permute-done.1.refs_2_, f32[8,104,128]{2,1,0:T(8,128)} %all-to-all-done.group_hbm.refs_3_, ...), custom_call_target="tpu_custom_call" | custom-call | tf_op jit(solution)/shard_map/down/pallas_call | solution.py:635
Async XLA Ops:
  3.0 14.5 %all-to-all-start = ((f32[8,104,128]{2,1,0:T(8,128)}), f32[8,104,128]{2,1,0:T(8,128)}, u32[]{:S(2)}, u32[]{:S(2)}) async-start(f32[8,104,128]{2,1,0:T(8,128)} %get-tuple-element.21), calls=%async_computation | async-start | bytes 851968 | tf_op jit(solution)/shard_map/all_to_all | solution.py:517
  19.8 11.1 %collective-permute-start.2 = (f32[376,128]{1,0:T(8,128)}, f32[376,128]{1,0:T(8,128)}, u32[]{:S(2)}, u32[]{:S(2)}) collective-permute-start(f32[376,128]{1,0:T(8,128)} %get-tuple-element.26), channel_id=1, source_target_pairs={{24,0},{25,1},{26,2},{27,3},{12,4},{13,5},{14,6},{15,7},{0,8},{1,9... | collective-permute-start | bytes 577544 | tf_op jit(solution)/shard_map/ppermute | solution.py:610
  21.8 9.0 %collective-permute-start.1 = (f32[1,7,8,128]{3,2,1,0:T(8,128)}, f32[1,7,8,128]{3,2,1,0:T(8,128)}, u32[]{:S(2)}, u32[]{:S(2)}) collective-permute-start(f32[1,7,8,128]{3,2,1,0:T(8,128)} %get-tuple-element.25.refs_0_), channel_id=1, source_target_pairs={{16,0},{17,1},{18,2},{19,3},{20,4},{21,5},{22,6},{23,7},{24,8},{25... | collective-permute-start | bytes 86024 | tf_op jit(solution)/shard_map/ppermute | solution.py:610
  24.4 6.4 %collective-permute-start = (f32[1,7,8,128]{3,2,1,0:T(8,128)}, f32[1,7,8,128]{3,2,1,0:T(8,128)}, u32[]{:S(2)}, u32[]{:S(2)}) collective-permute-start(f32[1,7,8,128]{3,2,1,0:T(8,128)} %get-tuple-element.25.refs_0_), channel_id=1, source_target_pairs={{8,0},{9,1},{10,2},{11,3},{28,4},{29,5},{30,6},{31,7},{16,8},{17,9... | collective-permute-start | bytes 86024 | tf_op jit(solution)/shard_map/ppermute | solution.py:610

commit v2 on v1

--- a/solution.py
+++ b/solution.py
@@ -41,6 +41,23 @@
     )
     cross = lax.dot_general(a_high, b_low, dims, preferred_element_type=F32)
     return both[:rows] + (both[rows:] + cross)
+
+
+def pair_dot(a, b, w_high, w_low):
+    a_high, a_low = halves(a)
+    b_high, b_low = halves(b)
+    rows = a.shape[0]
+    both = lax.dot_general(
+        jnp.concatenate([a_high, b_high, a_low, b_low], axis=0),
+        w_high,
+        NN,
+        preferred_element_type=F32,
+    )
+    cross = lax.dot_general(
+        jnp.concatenate([a_high, b_high], axis=0), w_low, NN, preferred_element_type=F32
+    )
+    total = both[: 2 * rows] + (both[2 * rows :] + cross)
+    return total[:rows], total[rows:]
 
 
 def dot3(a, b, dims):
@@ -128,144 +145,137 @@
             out[peer, rows, :] = jnp.where(above, last, first)
 
 
-def side_kernel(me_ref, *refs):
-    inputs, outputs = refs[:11], refs[11:23]
-    held, results = refs[23:34], refs[34:46]
-    sems, leaf_sems, out_sems, leaf_out_sems = refs[46:]
-    ids_s, links_s, transfer_v, couple_v, x_ref, top_v, lift_v, order_v, far_v, bases_v, blocks_v = held
-    (
-        inverse_out,
-        up_high,
-        up_low,
-        path_high,
-        path_low,
-        near_out,
-        edge_high,
-        edge_low,
-        leaf_high,
-        leaf_low,
-        bases_high,
-        bases_low,
-    ) = results
+def near_kernel(me_ref, *refs):
+    inputs, outputs = refs[:4], refs[4:9]
+    held, results = refs[9:13], refs[13:18]
+    sems, block_sems, out_sems = refs[18:]
+    ids_s, x_v, transfer_v, blocks_v = held
+    near_out, up_high, up_low, edge_high, edge_low = results
     leaf_dev, slots, leaf_size, _ = blocks_v.shape
-    _, rank, _ = bases_v.shape
-    copies = fetch(list(zip(inputs[:8], held[:8])), sems)
-    by_leaf = [
-        fetch([(x.at[leaf], v.at[leaf]) for x, v in zip(inputs[8:], held[8:])], leaf_sems.at[leaf])
-        for leaf in range(leaf_dev)
-    ]
-    writes = []
-
-    def write(*indices):
-        for index in indices:
-            writes.extend(
-                fetch([(results[index], outputs[index])], out_sems.at[pl.ds(index, 1)])
+    vectors = x_v.shape[1]
+    rank = transfer_v.shape[2]
+    me = me_ref[0]
+    copies = fetch(list(zip(inputs[:3], held[:3])), sems)
+
+    def block(leaf):
+        return pltpu.make_async_copy(inputs[3].at[leaf], blocks_v.at[leaf], block_sems.at[leaf])
+
+    for leaf in range(leaf_dev):
+        block(leaf).start()
+    for copy in copies:
+        copy.wait()
+    columns = leaf_dev * vectors
+    x_high, x_low = halves(x_v[...].reshape(columns, leaf_size).T)
+    x_both = jnp.concatenate([x_high, x_low], axis=1)
+    owner = lax.broadcasted_iota(jnp.int32, (leaf_size, columns), 1) // vectors
+
+    composed = transfer_v[0].reshape(2 * rank, rank)
+    row = 0
+    for level in range(1, DEPTH):
+        rows = composed.shape[0]
+        up_high[row : row + rows], up_low[row : row + rows] = halves(composed)
+        row += rows
+        if level < DEPTH - 1:
+            composed = jnp.concatenate(
+                [dot3(composed, transfer_v[level, side], NN) for side in range(2)], axis=0
             )
-
-    me = me_ref[0]
-    bits = [lax.shift_right_logical(me, level) & 1 for level in range(DEPTH)]
-
-    def put_up(row, weights):
-        span = slice(row, row + weights.shape[0])
-        up_high[span], up_low[span] = halves(weights)
-
-    def put_path(column, weights):
-        span = slice(column * rank, column * rank + weights.shape[1])
-        path_high[:, span], path_low[:, span] = halves(weights)
-
-    def couplings(level):
-        return jnp.concatenate(
-            [
-                links_s[level, column].astype(F32) * couple_v[level, column]
-                for column in range(len(OFFSETS))
-            ],
-            axis=1,
-        )
-
-    def inverse():
-        points_dev = order_v.shape[1]
-        tiles = points_dev // LANES
-        spot = order_v[...] - me * points_dev
-        times = lax.broadcasted_iota(jnp.int32, (1, points_dev), 1)
-        shape = (tiles, points_dev)
-        match = lax.broadcasted_iota(jnp.int32, shape, 0) == lax.shift_right_logical(spot, 7)
-        digits = [
-            jnp.where(match, jnp.broadcast_to(digit.astype(F32), shape), 0.0)
-            for digit in (lax.shift_right_logical(times, 4), times & 15)
-        ]
-        shape = (LANES, points_dev)
-        match = lax.broadcasted_iota(jnp.int32, shape, 0) == (spot & (LANES - 1))
-        both = lax.dot_general(
-            jnp.concatenate(digits, axis=0).astype(BF16),
-            jnp.where(match, 1.0, 0.0).astype(BF16),
-            NT,
-            preferred_element_type=F32,
-        )
-        inverse_out[...] = (both[:tiles] * 16.0 + both[tiles:]).astype(jnp.int32)
-
-    def edge(index, leaf, outside):
+    writes = fetch([(results[k], outputs[k]) for k in (1, 2)], out_sems)
+
+    def leaf_step(leaf, carry):
+        block(leaf).wait()
+        total = jnp.zeros((leaf_size, columns), F32)
+        for slot in range(slots):
+            high, low = halves(blocks_v[leaf, slot])
+            wide = lax.dot_general(high, x_both, NN, preferred_element_type=F32)
+            cross = lax.dot_general(low, x_high, NN, preferred_element_type=F32)
+            product = wide[:, :columns] + (wide[:, columns:] + cross)
+            total = total + jnp.where(owner == ids_s[slot, leaf] - me * leaf_dev, product, 0.0)
+        parts = total.T
+        result = parts[:vectors]
+        for other in range(1, leaf_dev):
+            result = result + parts[other * vectors : (other + 1) * vectors]
+        near_out[leaf] = result
+        return carry
+
+    lax.fori_loop(0, leaf_dev, leaf_step, 0)
+
+    for index, leaf, outside in ((0, 0, -1), (1, leaf_dev - 1, leaf_dev)):
         total = jnp.zeros((leaf_size, leaf_size), F32)
         for slot in range(1, slots):
             remote = ids_s[slot, leaf] - me * leaf_dev == outside
             total = total + jnp.where(remote, blocks_v[leaf, slot], 0.0)
-        edge_high[index], edge_low[index] = halves(total)
-
-    def chain():
-        up = transfer_v[0].reshape(2 * rank, rank)
-        path = transfer_v[0, bits[0]]
-        put_up(0, up)
-        put_path(0, couplings(0))
-        row = up.shape[0]
-        for level in range(1, DEPTH):
-            yield
-            if level < DEPTH - 1:
-                up = jnp.concatenate(
-                    [dot3(up, transfer_v[level, side], NN) for side in range(2)], axis=0
-                )
-                put_up(row, up)
-                row += up.shape[0]
-            put_path(level * len(OFFSETS), dot3(path, couplings(level), NN))
-            path = dot3(path, transfer_v[level, bits[level]], NN)
-        write(1, 2)
-        yield
-        top = dot3(path, top_v[...], NN)
-        yield
-        last = [dot3(top, transfer_v[DEPTH - 1, side], NT) for side in range(2)]
-        put_path(DEPTH * len(OFFSETS), jnp.concatenate(last, axis=1))
-        write(3, 4)
-        yield
-        inverse()
-        write(0)
-
-    links = chain()
+        edge_high[index], edge_low[index] = halves(total.T)
+    writes += fetch([(results[k], outputs[k]) for k in (0, 3, 4)], out_sems.at[pl.ds(2, 3)])
+    for copy in writes:
+        copy.wait()
+
+
+def weight_kernel(me_ref, *refs):
+    inputs, outputs = refs[:8], refs[8:15]
+    held, results = refs[15:23], refs[23:30]
+    sems, out_sems = refs[30:]
+    links_s, transfer_v, couple_v, top_v, lift_v, far_v, bases_v, order_v = held
+    path_high, path_low, leaf_high, leaf_low, bases_high, bases_low, inverse_out = results
+    copies = fetch(list(zip(inputs, held)), sems)
+    me = me_ref[0]
+    pairs, leaf_rows, _ = leaf_high.shape
+    rank = top_v.shape[0]
+    slots = far_v.shape[1]
     for copy in copies:
         copy.wait()
-    for leaf in range(leaf_dev):
-        for copy in by_leaf[leaf]:
-            copy.wait()
-        total = jnp.zeros(near_out.shape[1:], F32)
-        for slot in range(slots):
-            local = ids_s[slot, leaf] - me * leaf_dev
-            here = (local >= 0) & (local < leaf_dev)
-            x_leaf = jnp.where(here, x_ref[jnp.clip(local, 0, leaf_dev - 1)], 0.0)
-            total = total + dot3(x_leaf, blocks_v[leaf, slot], NT)
-        near_out[leaf] = total
-        row = [far_v[leaf, slot] for slot in range(far_v.shape[1])] + [lift_v[leaf]]
-        leaf_high[leaf], leaf_low[leaf] = halves(jnp.concatenate(row, axis=1))
-        bases_high[leaf], bases_low[leaf] = halves(bases_v[leaf])
-        if leaf == 0:
-            edge(0, leaf, -1)
-        if leaf == leaf_dev - 1:
-            edge(1, leaf, leaf_dev)
-        next(links, None)
-        writes += fetch(
-            [(v.at[leaf], x.at[leaf]) for v, x in zip(results[8:], outputs[8:])],
-            leaf_out_sems.at[leaf],
-        )
-    for _ in links:
-        pass
-    write(5, 6, 7)
-    for copy in writes:
+
+    path = None
+    blocks = []
+    for level in range(DEPTH):
+        weights = [
+            links_s[level, column].astype(F32) * couple_v[level, column]
+            for column in range(len(OFFSETS))
+        ]
+        weights = jnp.concatenate(weights, axis=1)
+        step = transfer_v[level, lax.shift_right_logical(me, level) & 1]
+        if path is not None:
+            weights = dot3(path, weights, NN)
+            step = dot3(path, step, NN)
+        path = step
+        blocks += [weights[:, k * rank : (k + 1) * rank] for k in range(len(OFFSETS))]
+    top = dot3(path, top_v[...], NN)
+    blocks += [dot3(top, transfer_v[DEPTH - 1, side], NT) for side in range(2)]
+    half = len(blocks) // 2
+    for index in range(half):
+        span = slice(index * rank, (index + 1) * rank)
+        both = jnp.concatenate([blocks[index], blocks[half + index]], axis=0).T
+        path_high[span], path_low[span] = halves(both)
+
+    for pair in range(pairs):
+        for slot in range(slots + 1):
+            two = [
+                lift_v[2 * pair + k] if slot == slots else far_v[2 * pair + k, slot]
+                for k in range(2)
+            ]
+            span = slice(slot * rank, (slot + 1) * rank)
+            leaf_high[pair, span], leaf_low[pair, span] = halves(jnp.concatenate(two, axis=0).T)
+        bases_high[pair], bases_low[pair] = halves(bases_v[pair])
+
+    points_dev = order_v.shape[1]
+    tiles = points_dev // LANES
+    spot = order_v[...] - me * points_dev
+    times = lax.broadcasted_iota(jnp.int32, (1, points_dev), 1)
+    shape = (tiles, points_dev)
+    match = lax.broadcasted_iota(jnp.int32, shape, 0) == lax.shift_right_logical(spot, 7)
+    digits = [
+        jnp.where(match, jnp.broadcast_to(digit.astype(F32), shape), 0.0)
+        for digit in (lax.shift_right_logical(times, 4), times & 15)
+    ]
+    shape = (LANES, points_dev)
+    match = lax.broadcasted_iota(jnp.int32, shape, 0) == (spot & (LANES - 1))
+    both = lax.dot_general(
+        jnp.concatenate(digits, axis=0).astype(BF16),
+        jnp.where(match, 1.0, 0.0).astype(BF16),
+        NT,
+        preferred_element_type=F32,
+    )
+    inverse_out[...] = (both[:tiles] * 16.0 + both[tiles:]).astype(jnp.int32)
+    for copy in fetch(list(zip(results, outputs)), out_sems):
         copy.wait()
 
 
@@ -381,6 +391,7 @@
     points_dev = out_ref.shape[1]
     slots = far_ids_s.shape[1]
     per_leaf = leaf_size // LANES
+    rank = bases_high.shape[1] // 2
     start = (leaf_dev + 1) * TILE
     edge_rows = group_ref.shape[1] - start
 
@@ -420,7 +431,12 @@
             weight = jnp.where(distance >= 2, 1.0 / jnp.maximum(distance, 1).astype(F32), 0.0)
             blended = blended + weight * nodes_ref[2 * other + side, GROUP - 2]
         partners.append(blended)
-    down = dot_halves(row_of(partners), path_high[...], path_low[...], NT)
+    half = len(partners) // 2
+    row = row_of(partners)
+    first, second = pair_dot(
+        row[:, : half * rank], row[:, half * rank :], path_high[...], path_low[...]
+    )
+    down = first[:, :rank] + second[:, rank:]
 
     for copy in copies[4:8]:
         copy.wait()
@@ -436,26 +452,33 @@
             )
         )
     edge_parts = [
-        dot_halves(edges[index], edge_high[index], edge_low[index], NT) for index in range(2)
+        dot_halves(edges[index], edge_high[index], edge_low[index], NN) for index in range(2)
     ]
 
     for copy in copies[8:]:
         copy.wait()
-    for leaf in range(leaf_dev):
-        picked = []
-        for slot in range(slots):
-            used = slot < far_count_s[leaf]
-            spot = far_ids_s[leaf, slot]
-            tile = tile_of(lax.shift_right_logical(spot, 3), spot & (leaf_dev - 1))
-            picked.append(jnp.where(used, tile, 0.0))
-        left = jnp.concatenate([row_of(picked), down], axis=1)
-        leaf_out = dot_halves(left, leaf_high[leaf], leaf_low[leaf], NT)
-        y_leaf = near_ref[leaf] + dot_halves(leaf_out, bases_high[leaf], bases_low[leaf], NN)
-        if leaf == 0:
-            y_leaf = y_leaf + edge_parts[0]
-        if leaf == leaf_dev - 1:
-            y_leaf = y_leaf + edge_parts[1]
-        y_tree[:, leaf * leaf_size : (leaf + 1) * leaf_size] = y_leaf
+    left_half = lax.broadcasted_iota(jnp.int32, (vectors, 2 * rank), 1) < rank
+    for pair in range(leaf_dev // 2):
+        rows = []
+        for leaf in (2 * pair, 2 * pair + 1):
+            picked = []
+            for slot in range(slots):
+                used = slot < far_count_s[leaf]
+                spot = far_ids_s[leaf, slot]
+                tile = tile_of(lax.shift_right_logical(spot, 3), spot & (leaf_dev - 1))
+                picked.append(jnp.where(used, tile, 0.0))
+            rows.append(jnp.concatenate([row_of(picked), down], axis=1))
+        first, second = pair_dot(*rows, leaf_high[pair], leaf_low[pair])
+        first = jnp.where(left_half, first, 0.0)
+        second = jnp.where(left_half, 0.0, second)
+        parts = pair_dot(first, second, bases_high[pair], bases_low[pair])
+        for leaf, part in zip((2 * pair, 2 * pair + 1), parts):
+            y_leaf = near_ref[leaf] + part
+            if leaf == 0:
+                y_leaf = y_leaf + edge_parts[0]
+            if leaf == leaf_dev - 1:
+                y_leaf = y_leaf + edge_parts[1]
+            y_tree[:, leaf * leaf_size : (leaf + 1) * leaf_size] = y_leaf
 
     y = y_tree[...]
     for tile in range(points_dev // LANES):
@@ -517,70 +540,56 @@
     group_in = lax.all_to_all(group_out, "leaf", 0, 0, axis_index_groups=aligned, tiled=True)
 
     ids_t = near_ids.T
+    both = lambda *size: [shape(size, BF16)] * 2
+
+    def call(kernel, operands, results, scalar, sems, cost, name):
+        return pl.pallas_call(
+            kernel,
+            out_shape=results,
+            in_specs=[SMEM] + [HBM] * len(operands),
+            out_specs=[HBM] * len(results),
+            scratch_shapes=[
+                (pltpu.SMEM if x is scalar else pltpu.VMEM)(x.shape, x.dtype) for x in operands
+            ]
+            + [pltpu.VMEM(x.shape, x.dtype) for x in results]
+            + [pltpu.SemaphoreType.DMA((count,)) for count in sems],
+            compiler_params=PARAMS,
+            cost_estimate=pl.CostEstimate(flops=cost * 250, bytes_accessed=cost, transcendentals=0),
+            name=name,
+        )(me, *operands)
+
+    near_part, up_high, up_low, edge_high, edge_low = call(
+        near_kernel,
+        (ids_t, tree_x, transfer, near_blocks),
+        [shape(tree_x.shape, F32)] + both(14 * rank, rank) + both(2, leaf_size, leaf_size),
+        ids_t,
+        (3, leaf_dev, 5),
+        12_000_000,
+        "near",
+    )
     links_own = links.reshape(links.shape[1:])
-    composed_rows = (2 + 4 + 8) * rank
-    path_columns = (DEPTH * len(OFFSETS) + 2) * rank
-    leaf_columns = (far_slots + 1) * rank
-    both = lambda *size: [shape(size, BF16)] * 2
-    operands = (
-        ids_t,
+    path_rows = (DEPTH * len(OFFSETS) + 2) // 2 * rank
+    path_high, path_low, leaf_high, leaf_low, bases_high, bases_low, inverse = call(
+        weight_kernel,
+        (
+            links_own,
+            transfer,
+            couple,
+            top_couple,
+            lift,
+            far_blocks,
+            bases_t.reshape(leaf_dev // 2, 2 * rank, leaf_size),
+            order.reshape(1, points_dev),
+        ),
+        both(path_rows, 2 * rank)
+        + both(leaf_dev // 2, (far_slots + 1) * rank, 2 * rank)
+        + both(leaf_dev // 2, 2 * rank, leaf_size)
+        + [shape((tiles, LANES), jnp.int32)],
         links_own,
-        transfer,
-        couple,
-        tree_x,
-        top_couple,
-        lift,
-        order.reshape(1, points_dev),
-        far_blocks,
-        bases_t,
-        near_blocks,
-    )
-    results = (
-        [shape((tiles, LANES), jnp.int32)]
-        + both(composed_rows, rank)
-        + both(rank, path_columns)
-        + [shape(tree_x.shape, F32)]
-        + both(2, leaf_size, leaf_size)
-        + both(leaf_dev, rank, leaf_columns)
-        + both(leaf_dev, rank, leaf_size)
-    )
-    (
-        inverse,
-        up_high,
-        up_low,
-        path_high,
-        path_low,
-        near_part,
-        edge_high,
-        edge_low,
-        leaf_high,
-        leaf_low,
-        bases_high,
-        bases_low,
-    ) = pl.pallas_call(
-        side_kernel,
-        out_shape=results,
-        in_specs=[SMEM] + [HBM] * len(operands),
-        out_specs=[HBM] * len(results),
-        scratch_shapes=[
-            (pltpu.SMEM if x is ids_t or x is links_own else pltpu.VMEM)(x.shape, x.dtype)
-            for x in operands
-        ]
-        + [pltpu.VMEM(x.shape, x.dtype) for x in results]
-        + [
-            pltpu.SemaphoreType.DMA((8,)),
-            pltpu.SemaphoreType.DMA((leaf_dev, 3)),
-            pltpu.SemaphoreType.DMA((8,)),
-            pltpu.SemaphoreType.DMA((leaf_dev, 4)),
-        ],
-        compiler_params=PARAMS,
-        cost_estimate=pl.CostEstimate(
-            flops=6 * vectors * near_blocks.size,
-            bytes_accessed=4 * near_blocks.size,
-            transcendentals=0,
-        ),
-        name="side",
-    )(me, *operands)
+        (8, 7),
+        12_000_000,
+        "weights",
+    )
 
     by_permute = groups == 4
     half_out, nodes_out = pl.pallas_call(

time: 36.4 us -> 36.6 us (level)
  Pallas kernels: 19.9 us -> 23 us
  waiting for transfers between devices: 5.1 us -> 3.13 us
  starting transfers between devices: 11.2 us -> 10.2 us
    pallas_call x1 -> x2, Pallas kernels: 9.29 us -> 12.9 us  [call(): pl.pallas_call(kernel, out_shape=results, in_specs=[SMEM] + [HBM] * len(o...]
    ppermute x3, waiting for transfers between devices: 5.09 us -> 2.3 us  [shifted(): return lax.ppermute(x, 'leaf', pairs)]
    ppermute x3, starting transfers between devices: 5.98 us -> 4.96 us  [shifted(): return lax.ppermute(x, 'leaf', pairs)]
    all_to_all x1, waiting for transfers between devices: 0.01 us -> 0.84 us  [local(): lax.all_to_all(group_out, 'leaf', 0, 0, axis_index_groups=aligned, tiled=...]
    pallas_call x1, Pallas kernels: 5.32 us -> 4.85 us  [local(): pl.pallas_call(functools.partial(down_kernel, len(node_parts)), out_shape...]
  transfers between devices with their start and end apart: 4 -> 4, of which waited for: 1 -> 2; matrix products, arithmetic and copies ran while one was open for 0% -> 0% of each run, Pallas kernels for 26% -> 36%
where the time goes in v2:
time: 36.6 us; the launch traced here: 36.3 us
  Pallas kernels  23 us (63%)
  starting transfers between devices  10.2 us (28%)
  waiting for transfers between devices  3.13 us (9%)
    pallas_call x2, Pallas kernels, call(): pl.pallas_call(kernel, out_shape=results, in_specs=[SMEM] + [HBM] * len(o...  12.9 us
    all_to_all x1, starting transfers between devices, local(): lax.all_to_all(group_out, 'leaf', 0, 0, axis_index_groups=aligned, tiled=...  5.19 us
    ppermute x3, starting transfers between devices, shifted(): return lax.ppermute(x, 'leaf', pairs)  4.96 us
    pallas_call x1, Pallas kernels, local(): pl.pallas_call(functools.partial(down_kernel, len(node_parts)), out_shape...  4.85 us
    pallas_call x1, Pallas kernels, local(): pl.pallas_call(up_kernel, out_shape=[shape((GROUP, rows + edge_rows, LANE...  2.98 us
    ppermute x3, waiting for transfers between devices, shifted(): return lax.ppermute(x, 'leaf', pairs)  2.3 us
    pallas_call x1, Pallas kernels, local(): pl.pallas_call(functools.partial(middle_kernel, leaf_dev), out_shape=[sha...  2.24 us
    all_to_all x1, waiting for transfers between devices, local(): lax.all_to_all(group_out, 'leaf', 0, 0, axis_index_groups=aligned, tiled=...  0.84 us
  transfers between devices with their start and end apart: 4, of which 2 were waited for; matrix products, arithmetic and copies ran while one was open for 0% of the time, Pallas kernels for 36%

profile of v2, /device:TPU:0, one launch (start us, length us, event | category | flops | bytes accessed | tf_op | source)
XLA Modules:
  0.0 36.3 jit_solution(15858821721816636948)
XLA Ops:
  0.0 3.0 %up.1 = (f32[8,104,128]{2,1,0:T(8,128)}, f32[8,16,256]{2,1,0:T(8,128)}) custom-call(s32[1]{0:T(128)} %bitcast.me_ref, f32[16,2048]{1,0:T(8,128)} %points_hbm.1, s32[16,128]{1,0:T(8,128)} %bitcast.10, f32[8,64,256]{2,1,0:T(8,128)} %bitcast.8, f32[8,64,64]{2,1,0:T(8,128)} %refs_4_.1), custom_call_target="tpu_custom_call" | custom-call | tf_op jit(solution)/shard_map/up/pallas_call | solution.py:520
  3.0 5.2 %all-to-all-start = ((f32[8,104,128]{2,1,0:T(8,128)}), f32[8,104,128]{2,1,0:T(8,128)}, u32[]{:S(2)}, u32[]{:S(2)}) async-start(f32[8,104,128]{2,1,0:T(8,128)} %get-tuple-element.21), calls=%async_computation | async-start | bytes 851968 | tf_op jit(solution)/shard_map/all_to_all | solution.py:540
  8.2 8.0 %near.1 = (f32[8,16,256]{2,1,0:T(8,128)}, bf16[896,64]{1,0:T(8,128)(2,1)}, bf16[896,64]{1,0:T(8,128)(2,1)}, bf16[2,256,256]{2,1,0:T(8,128)(2,1)}, bf16[2,256,256]{2,1,0:T(8,128)(2,1)}) custom-call(s32[1]{0:T(128)} %bitcast.me_ref, s32[3,8]{1,0:T(4,128)} %bitcast.12, f32[8,16,256]{2,1,0:T(8,128)} %get-tuple-element.22.refs_1_, f32[4,2,64,64]{3,2,1,0:T(8,128)} %refs_1_.1, ...), custom_call_target="tpu_custom_call" | custom-call | flops 3000000000 | bytes 12000000 | tf_op jit(solution)/shard_map/near/pallas_call | solution.py:546
  16.1 0.8 %all-to-all-done.group_hbm.refs_3_ = f32[8,104,128]{2,1,0:T(8,128)} async-done(((f32[8,104,128]{2,1,0:T(8,128)}), f32[8,104,128]{2,1,0:T(8,128)}, u32[]{:S(2)}, u32[]{:S(2)}) %all-to-all-start) | async-done | bytes 426016 | tf_op jit(solution)/shard_map/all_to_all | solution.py:540
  17.0 2.2 %middle.1 = (f32[376,128]{1,0:T(8,128)}, f32[1,7,8,128]{3,2,1,0:T(8,128)}) custom-call(s32[1]{0:T(128)} %bitcast.me_ref, f32[8,104,128]{2,1,0:T(8,128)} %all-to-all-done.group_hbm.refs_3_, bf16[896,64]{1,0:T(8,128)(2,1)} %get-tuple-element.23.up_high_hbm, bf16[896,64]{1,0:T(8,128)(2,1)} %get-tuple-element.24.up_low_hbm), custom_call_target="tpu_custom_call" | custom-call | tf_op jit(solution)/shard_map/middle/pallas_call | solution.py:595
  19.2 2.9 %collective-permute-start.1 = (f32[1,7,8,128]{3,2,1,0:T(8,128)}, f32[1,7,8,128]{3,2,1,0:T(8,128)}, u32[]{:S(2)}, u32[]{:S(2)}) collective-permute-start(f32[1,7,8,128]{3,2,1,0:T(8,128)} %get-tuple-element.25.refs_0_), channel_id=1, source_target_pairs={{16,0},{17,1},{18,2},{19,3},{20,4},{21,5},{22,6},{23,7},{24,8},{25... | collective-permute-start | bytes 86024 | tf_op jit(solution)/shard_map/ppermute | solution.py:619
  22.2 1.3 %collective-permute-start = (f32[1,7,8,128]{3,2,1,0:T(8,128)}, f32[1,7,8,128]{3,2,1,0:T(8,128)}, u32[]{:S(2)}, u32[]{:S(2)}) collective-permute-start(f32[1,7,8,128]{3,2,1,0:T(8,128)} %get-tuple-element.25.refs_0_), channel_id=1, source_target_pairs={{8,0},{9,1},{10,2},{11,3},{28,4},{29,5},{30,6},{31,7},{16,8},{17,9... | collective-permute-start | bytes 86024 | tf_op jit(solution)/shard_map/ppermute | solution.py:619
  23.5 0.7 %collective-permute-start.2 = (f32[376,128]{1,0:T(8,128)}, f32[376,128]{1,0:T(8,128)}, u32[]{:S(2)}, u32[]{:S(2)}) collective-permute-start(f32[376,128]{1,0:T(8,128)} %get-tuple-element.26), channel_id=1, source_target_pairs={{24,0},{25,1},{26,2},{27,3},{12,4},{13,5},{14,6},{15,7},{0,8},{1,9... | collective-permute-start | bytes 577544 | tf_op jit(solution)/shard_map/ppermute | solution.py:619
  24.2 5.0 %weights.1 = (bf16[576,128]{1,0:T(8,128)(2,1)}, bf16[576,128]{1,0:T(8,128)(2,1)}, bf16[4,576,128]{2,1,0:T(8,128)(2,1)}, bf16[4,576,128]{2,1,0:T(8,128)(2,1)}, bf...) custom-call(s32[1]{0:T(128)} %bitcast.me_ref, s32[4,4]{1,0:T(4,128)} %bitcast.13, ...), custom_call_target="tpu_custom_call" | custom-call | flops 3000000000 | bytes 12000000 | tf_op jit(solution)/shard_map/weights/pallas_call | solution.py:546
  29.2 0.0 collective-permute-done.1.refs_2_
  29.2 0.0 collective-permute-done.refs_1_
  29.2 2.3 %collective-permute-done.2.refs_4_ = f32[376,128]{1,0:T(8,128)} collective-permute-done((f32[376,128]{1,0:T(8,128)}, f32[376,128]{1,0:T(8,128)}, u32[]{:S(2)}, u32[]{:S(2)}) %collective-permute-start.2) | collective-permute-done | bytes 192544 | tf_op jit(solution)/shard_map/ppermute | solution.py:619
  31.5 4.8 %down.1 = f32[16,2048]{1,0:T(8,128)} custom-call(s32[1]{0:T(128)} %bitcast.me_ref, f32[1,7,8,128]{3,2,1,0:T(8,128)} %get-tuple-element.25.refs_0_, f32[1,7,8,128]{3,2,1,0:T(8,128)} %collective-permute-done.refs_1_, f32[1,7,8,128]{3,2,1,0:T(8,128)} %collective-permute-done.1.refs_2_, f32[8,104,128]{2,1,0:T(8,128)} %all-to-all-done.group_hbm.refs_3_, ...), custom_call_target="tpu_custom_call" | custom-call | tf_op jit(solution)/shard_map/down/pallas_call | solution.py:644
Async XLA Ops:
  3.0 14.0 %all-to-all-start = ((f32[8,104,128]{2,1,0:T(8,128)}), f32[8,104,128]{2,1,0:T(8,128)}, u32[]{:S(2)}, u32[]{:S(2)}) async-start(f32[8,104,128]{2,1,0:T(8,128)} %get-tuple-element.21), calls=%async_computation | async-start | bytes 851968 | tf_op jit(solution)/shard_map/all_to_all | solution.py:540
  19.2 10.0 %collective-permute-start.1 = (f32[1,7,8,128]{3,2,1,0:T(8,128)}, f32[1,7,8,128]{3,2,1,0:T(8,128)}, u32[]{:S(2)}, u32[]{:S(2)}) collective-permute-start(f32[1,7,8,128]{3,2,1,0:T(8,128)} %get-tuple-element.25.refs_0_), channel_id=1, source_target_pairs={{16,0},{17,1},{18,2},{19,3},{20,4},{21,5},{22,6},{23,7},{24,8},{25... | collective-permute-start | bytes 86024 | tf_op jit(solution)/shard_map/ppermute | solution.py:619
  22.2 7.0 %collective-permute-start = (f32[1,7,8,128]{3,2,1,0:T(8,128)}, f32[1,7,8,128]{3,2,1,0:T(8,128)}, u32[]{:S(2)}, u32[]{:S(2)}) collective-permute-start(f32[1,7,8,128]{3,2,1,0:T(8,128)} %get-tuple-element.25.refs_0_), channel_id=1, source_target_pairs={{8,0},{9,1},{10,2},{11,3},{28,4},{29,5},{30,6},{31,7},{16,8},{17,9... | collective-permute-start | bytes 86024 | tf_op jit(solution)/shard_map/ppermute | solution.py:619
  23.5 8.0 %collective-permute-start.2 = (f32[376,128]{1,0:T(8,128)}, f32[376,128]{1,0:T(8,128)}, u32[]{:S(2)}, u32[]{:S(2)}) collective-permute-start(f32[376,128]{1,0:T(8,128)} %get-tuple-element.26), channel_id=1, source_target_pairs={{24,0},{25,1},{26,2},{27,3},{12,4},{13,5},{14,6},{15,7},{0,8},{1,9... | collective-permute-start | bytes 577544 | tf_op jit(solution)/shard_map/ppermute | solution.py:619

commit v3 on v2

--- a/solution.py
+++ b/solution.py
@@ -107,7 +107,20 @@
 
 
 def up_kernel(
-    me_ref, points_hbm, order_hbm, bases_hbm, lift_hbm, out, x_out, points_v, order_v, bases_v, lift_v, sems
+    me_ref,
+    points_hbm,
+    order_hbm,
+    bases_hbm,
+    lift_hbm,
+    out,
+    x_out,
+    first_out,
+    last_out,
+    points_v,
+    order_v,
+    bases_v,
+    lift_v,
+    sems,
 ):
     copies = fetch(
         [(order_hbm, order_v), (points_hbm, points_v), (bases_hbm, bases_v), (lift_hbm, lift_v)], sems
@@ -134,21 +147,14 @@
     for peer in range(GROUP):
         for index, tile in enumerate(tiles):
             out[peer, index * TILE : (index + 1) * TILE, :] = tile
-    place = lax.rem(me, GROUP)
-    start = len(tiles) * TILE
-    for part in range(per_leaf):
-        first = x_out[0, :, part * LANES : (part + 1) * LANES]
-        last = x_out[leaf_dev - 1, :, part * LANES : (part + 1) * LANES]
-        rows = slice(start + part * vectors, start + (part + 1) * vectors)
-        for peer in range(GROUP):
-            above = lax.rem(place + 1, GROUP) == peer
-            out[peer, rows, :] = jnp.where(above, last, first)
+    first_out[...] = x_out[0]
+    last_out[...] = x_out[leaf_dev - 1]
 
 
 def near_kernel(me_ref, *refs):
     inputs, outputs = refs[:4], refs[4:9]
     held, results = refs[9:13], refs[13:18]
-    sems, block_sems, out_sems = refs[18:]
+    product_v, total_v, sems, block_sems, out_sems = refs[18:]
     ids_s, x_v, transfer_v, blocks_v = held
     near_out, up_high, up_low, edge_high, edge_low = results
     leaf_dev, slots, leaf_size, _ = blocks_v.shape
@@ -165,9 +171,9 @@
     for copy in copies:
         copy.wait()
     columns = leaf_dev * vectors
-    x_high, x_low = halves(x_v[...].reshape(columns, leaf_size).T)
-    x_both = jnp.concatenate([x_high, x_low], axis=1)
-    owner = lax.broadcasted_iota(jnp.int32, (leaf_size, columns), 1) // vectors
+    x_both = jnp.concatenate(halves(x_v[...].reshape(columns, leaf_size).T), axis=1)
+    chunk = 64
+    owner = lax.broadcasted_iota(jnp.int32, (chunk, columns), 1) // vectors
 
     composed = transfer_v[0].reshape(2 * rank, rank)
     row = 0
@@ -183,14 +189,23 @@
 
     def leaf_step(leaf, carry):
         block(leaf).wait()
-        total = jnp.zeros((leaf_size, columns), F32)
+        left = []
         for slot in range(slots):
-            high, low = halves(blocks_v[leaf, slot])
-            wide = lax.dot_general(high, x_both, NN, preferred_element_type=F32)
-            cross = lax.dot_general(low, x_high, NN, preferred_element_type=F32)
-            product = wide[:, :columns] + (wide[:, columns:] + cross)
-            total = total + jnp.where(owner == ids_s[slot, leaf] - me * leaf_dev, product, 0.0)
-        parts = total.T
+            left += halves(blocks_v[leaf, slot])
+        product_v[...] = lax.dot_general(
+            jnp.concatenate(left, axis=0), x_both, NN, preferred_element_type=F32
+        )
+        local = [ids_s[slot, leaf] - me * leaf_dev for slot in range(slots)]
+        for start in range(0, leaf_size, chunk):
+            total = jnp.zeros((chunk, columns), F32)
+            for slot in range(slots):
+                high = 2 * slot * leaf_size + start
+                low = high + leaf_size
+                wide = product_v[high : high + chunk] + product_v[low : low + chunk]
+                product = wide[:, :columns] + wide[:, columns:]
+                total = total + jnp.where(owner == local[slot], product, 0.0)
+            total_v[start : start + chunk] = total
+        parts = total_v[...].T
         result = parts[:vectors]
         for other in range(1, leaf_dev):
             result = result + parts[other * vectors : (other + 1) * vectors]
@@ -221,7 +236,7 @@
     pairs, leaf_rows, _ = leaf_high.shape
     rank = top_v.shape[0]
     slots = far_v.shape[1]
-    for copy in copies:
+    for copy in copies[:4]:
         copy.wait()
 
     path = None
@@ -246,6 +261,10 @@
         both = jnp.concatenate([blocks[index], blocks[half + index]], axis=0).T
         path_high[span], path_low[span] = halves(both)
 
+    writes = fetch([(results[k], outputs[k]) for k in range(2)], out_sems)
+    for copy in copies[4:]:
+        copy.wait()
+
     for pair in range(pairs):
         for slot in range(slots + 1):
             two = [
@@ -255,6 +274,8 @@
             span = slice(slot * rank, (slot + 1) * rank)
             leaf_high[pair, span], leaf_low[pair, span] = halves(jnp.concatenate(two, axis=0).T)
         bases_high[pair], bases_low[pair] = halves(bases_v[pair])
+
+    writes += fetch([(results[k], outputs[k]) for k in range(2, 6)], out_sems.at[pl.ds(2, 4)])
 
     points_dev = order_v.shape[1]
     tiles = points_dev // LANES
@@ -275,7 +296,8 @@
         preferred_element_type=F32,
     )
     inverse_out[...] = (both[:tiles] * 16.0 + both[tiles:]).astype(jnp.int32)
-    for copy in fetch(list(zip(results, outputs)), out_sems):
+    writes += fetch([(inverse_out, outputs[6])], out_sems.at[pl.ds(6, 1)])
+    for copy in writes:
         copy.wait()
 
 
@@ -285,6 +307,8 @@
     group_hbm,
     up_high_hbm,
     up_low_hbm,
+    below_hbm,
+    above_hbm,
     half_out,
     nodes_out,
     roots_v,
@@ -293,6 +317,7 @@
     sems,
     half_sems,
 ):
+    del below_hbm, above_hbm
     low = lax.rem(me_ref[0], GROUP) < REACH
     copies = fetch(
         [
@@ -303,18 +328,11 @@
         sems,
     )
     rows = (leaf_dev + 1) * TILE
-    edge_rows = group_hbm.shape[1] - rows
     first = jnp.where(low, REACH, 0)
     moves = [
         (group_hbm.at[first + part, pl.ds(0, rows)], half_out.at[pl.ds(part * rows, rows)])
         for part in range(REACH)
     ]
-    moves.append(
-        (
-            group_hbm.at[jnp.where(low, GROUP - 1, 0), pl.ds(rows, edge_rows)],
-            half_out.at[pl.ds(REACH * rows, edge_rows)],
-        )
-    )
     moves = fetch(moves, half_sems)
     for copy in copies:
         copy.wait()
@@ -330,7 +348,7 @@
         nodes = dot_halves(left, up_high[start : start + size], up_low[start : start + size], NN)
         start += size
         tiles += [fold(nodes[n * 2 * TILE : (n + 1) * 2 * TILE]) for n in range(count)]
-    row = REACH * rows + edge_rows
+    row = REACH * rows
     for index, tile in enumerate(tiles):
         half_out[row + index * TILE : row + (index + 1) * TILE, :] = tile
         for peer in range(nodes_out.shape[0]):
@@ -378,6 +396,8 @@
         path_low,
         far_ids_s,
         far_count_s,
+        below_ref,
+        above_ref,
         edge_high,
         edge_low,
         leaf_high,
@@ -390,10 +410,8 @@
     leaf_dev, vectors, leaf_size = near_ref.shape
     points_dev = out_ref.shape[1]
     slots = far_ids_s.shape[1]
-    per_leaf = leaf_size // LANES
     rank = bases_high.shape[1] // 2
     start = (leaf_dev + 1) * TILE
-    edge_rows = group_ref.shape[1] - start
 
     def tile_of(subtree, index):
         other = subtree & (GROUP - 1)
@@ -438,24 +456,14 @@
     )
     down = first[:, :rank] + second[:, rank:]
 
-    for copy in copies[4:8]:
-        copy.wait()
-    edges = []
-    for index, offset in ((0, -1), (1, 1)):
-        other = me + offset
-        inside = lax.shift_right_arithmetic(other, 3) == group
-        here = group_ref[other & (GROUP - 1), start:, :]
-        chosen = jnp.where(inside, here, half_ref[REACH * start : REACH * start + edge_rows, :])
-        edges.append(
-            jnp.concatenate(
-                [chosen[part * vectors : (part + 1) * vectors] for part in range(per_leaf)], axis=1
-            )
-        )
+    for copy in copies[4:10]:
+        copy.wait()
     edge_parts = [
-        dot_halves(edges[index], edge_high[index], edge_low[index], NN) for index in range(2)
+        dot_halves(edge[...], edge_high[index], edge_low[index], NN)
+        for index, edge in enumerate((below_ref, above_ref))
     ]
 
-    for copy in copies[8:]:
+    for copy in copies[10:]:
         copy.wait()
     left_half = lax.broadcasted_iota(jnp.int32, (vectors, 2 * rank), 1) < rank
     for pair in range(leaf_dev // 2):
@@ -511,20 +519,21 @@
     far_slots = far_ids.shape[1]
     bases_t = jnp.swapaxes(bases, 1, 2)
     tiles = points_dev // LANES
-    edge_rows = vectors * (leaf_size // LANES)
     rows = (leaf_dev + 1) * TILE
     groups = devices // GROUP
     order_tiles = order.reshape(tiles, LANES)
     shape = jax.ShapeDtypeStruct
 
-    group_out, tree_x = pl.pallas_call(
+    group_out, tree_x, first_leaf, last_leaf = pl.pallas_call(
         up_kernel,
         out_shape=[
-            shape((GROUP, rows + edge_rows, LANES), F32),
+            shape((GROUP, rows, LANES), F32),
             shape((leaf_dev, vectors, leaf_size), F32),
+            shape((vectors, leaf_size), F32),
+            shape((vectors, leaf_size), F32),
         ],
         in_specs=[SMEM] + [HBM] * 4,
-        out_specs=[VMEM] * 2,
+        out_specs=[VMEM] * 4,
         scratch_shapes=[
             pltpu.VMEM(points.shape, F32),
             pltpu.VMEM((tiles, LANES), jnp.int32),
@@ -538,11 +547,14 @@
 
     aligned = [[g * GROUP + i for i in range(GROUP)] for g in range(groups)]
     group_in = lax.all_to_all(group_out, "leaf", 0, 0, axis_index_groups=aligned, tiled=True)
+    forward = [(i, i + 1) for i in range(devices - 1)]
+    below = lax.ppermute(last_leaf, "leaf", forward)
+    above = lax.ppermute(first_leaf, "leaf", [(target, source) for source, target in forward])
 
     ids_t = near_ids.T
     both = lambda *size: [shape(size, BF16)] * 2
 
-    def call(kernel, operands, results, scalar, sems, cost, name):
+    def call(kernel, operands, results, scalar, scratch, sems, cost, name):
         return pl.pallas_call(
             kernel,
             out_shape=results,
@@ -552,6 +564,7 @@
                 (pltpu.SMEM if x is scalar else pltpu.VMEM)(x.shape, x.dtype) for x in operands
             ]
             + [pltpu.VMEM(x.shape, x.dtype) for x in results]
+            + [pltpu.VMEM(size, F32) for size in scratch]
             + [pltpu.SemaphoreType.DMA((count,)) for count in sems],
             compiler_params=PARAMS,
             cost_estimate=pl.CostEstimate(flops=cost * 250, bytes_accessed=cost, transcendentals=0),
@@ -563,6 +576,7 @@
         (ids_t, tree_x, transfer, near_blocks),
         [shape(tree_x.shape, F32)] + both(14 * rank, rank) + both(2, leaf_size, leaf_size),
         ids_t,
+        ((2 * slots * leaf_size, 2 * leaf_dev * vectors), (leaf_size, leaf_dev * vectors)),
         (3, leaf_dev, 5),
         12_000_000,
         "near",
@@ -586,6 +600,7 @@
         + both(leaf_dev // 2, 2 * rank, leaf_size)
         + [shape((tiles, LANES), jnp.int32)],
         links_own,
+        (),
         (8, 7),
         12_000_000,
         "weights",
@@ -595,21 +610,21 @@
     half_out, nodes_out = pl.pallas_call(
         functools.partial(middle_kernel, leaf_dev),
         out_shape=[
-            shape((REACH * rows + edge_rows + NODES * TILE, LANES), F32),
+            shape((REACH * rows + NODES * TILE, LANES), F32),
             shape((1 if by_permute else groups, NODES, TILE, LANES), F32),
         ],
-        in_specs=[SMEM] + [HBM] * 3,
+        in_specs=[SMEM] + [HBM] * 5,
         out_specs=[VMEM] * 2,
         scratch_shapes=[
             pltpu.VMEM((GROUP, TILE, LANES), F32),
             pltpu.VMEM(up_high.shape, BF16),
             pltpu.VMEM(up_low.shape, BF16),
             pltpu.SemaphoreType.DMA((3,)),
-            pltpu.SemaphoreType.DMA((REACH + 1,)),
+            pltpu.SemaphoreType.DMA((REACH,)),
         ],
         compiler_params=PARAMS,
         name="middle",
-    )(me, group_in, up_high, up_low)
+    )(me, group_in, up_high, up_low, below, above)
 
     def shifted(x, low, high):
         pairs = []
@@ -632,6 +647,8 @@
         path_low,
         far_ids,
         far_count,
+        below,
+        above,
         edge_high,
         edge_low,
         leaf_high,

time: 36.6 us -> 42.7 us (1.17)
  starting transfers between devices: 10.2 us -> 17.6 us
  Pallas kernels: 23 us -> 22.1 us
  waiting for transfers between devices: 3.13 us -> 2.64 us
    ppermute x0 -> x2, starting transfers between devices: none -> 4.28 us  [the longest x1 3 us: local(): below = lax.ppermute(last_leaf, 'leaf', forward)]
    ppermute x3, starting transfers between devices: 4.96 us -> 8.11 us  [shifted(): return lax.ppermute(x, 'leaf', pairs)]
    pallas_call x2, Pallas kernels: 12.9 us -> 12.1 us  [call(): pl.pallas_call(kernel, out_shape=results, in_specs=[SMEM] + [HBM] * len(o...]
    all_to_all x1, waiting for transfers between devices: 0.84 us -> 0.01 us  [local(): lax.all_to_all(group_out, 'leaf', 0, 0, axis_index_groups=aligned, tiled=...]
  transfers between devices with their start and end apart: 4 -> 6, of which waited for: 2 -> 1; matrix products, arithmetic and copies ran while one was open for 0% -> 0% of each run, Pallas kernels for 36% -> 29%
where the time goes in v3:
time: 42.7 us; the launch traced here: 42.4 us
  Pallas kernels  22.1 us (52%)
  starting transfers between devices  17.6 us (41%)
  waiting for transfers between devices  2.64 us (6%)
    pallas_call x2, Pallas kernels, call(): pl.pallas_call(kernel, out_shape=results, in_specs=[SMEM] + [HBM] * len(o...  12.1 us
    ppermute x3, starting transfers between devices, shifted(): return lax.ppermute(x, 'leaf', pairs)  8.11 us
    all_to_all x1, starting transfers between devices, local(): lax.all_to_all(group_out, 'leaf', 0, 0, axis_index_groups=aligned, tiled=...  5.19 us
    pallas_call x1, Pallas kernels, local(): pl.pallas_call(functools.partial(down_kernel, len(node_parts)), out_shape...  4.89 us
    ppermute x1, starting transfers between devices, local(): below = lax.ppermute(last_leaf, 'leaf', forward)  3 us
    pallas_call x1, Pallas kernels, local(): pl.pallas_call(up_kernel, out_shape=[shape((GROUP, rows, LANES), F32), sh...  2.94 us
    ppermute x3, waiting for transfers between devices, shifted(): return lax.ppermute(x, 'leaf', pairs)  2.63 us
    pallas_call x1, Pallas kernels, local(): pl.pallas_call(functools.partial(middle_kernel, leaf_dev), out_shape=[sha...  2.2 us
  transfers between devices with their start and end apart: 6, of which 1 were waited for; matrix products, arithmetic and copies ran while one was open for 0% of the time, Pallas kernels for 29%

profile of v3, /device:TPU:0, one launch (start us, length us, event | category | flops | bytes accessed | tf_op | source)
XLA Modules:
  0.0 42.4 jit_solution(9166505405029808332)
XLA Ops:
  0.0 2.9 %up.1 = (f32[8,72,128]{2,1,0:T(8,128)}, f32[8,16,256]{2,1,0:T(8,128)}, f32[16,256]{1,0:T(8,128)}, f32[16,256]{1,0:T(8,128)}) custom-call(s32[1]{0:T(128)} %bitcast.me_ref, f32[16,2048]{1,0:T(8,128)} %points_hbm.1, s32[16,128]{1,0:T(8,128)} %bitcast.10, f32[8,64,256]{2,1,0:T(8,128)} %bitcast.8, f32[8,64,64]{2,1,0:T(8,128)} %refs_4_.1), custom_call_target="tpu_custom_call" | custom-call | tf_op jit(solution)/shard_map/up/pallas_call | solution.py:527
  2.9 5.2 %all-to-all-start = ((f32[8,72,128]{2,1,0:T(8,128)}), f32[8,72,128]{2,1,0:T(8,128)}, u32[]{:S(2)}, u32[]{:S(2)}) async-start(f32[8,72,128]{2,1,0:T(8,128)} %get-tuple-element.23), calls=%async_computation | async-start | bytes 589824 | tf_op jit(solution)/shard_map/all_to_all | solution.py:549
  8.1 3.0 %collective-permute-start = (f32[16,256]{1,0:T(8,128)}, f32[16,256]{1,0:T(8,128)}, u32[]{:S(2)}, u32[]{:S(2)}) collective-permute-start(f32[16,256]{1,0:T(8,128)} %get-tuple-element.27), channel_id=1, source_target_pairs={{0,1},{1,2},{2,3},{3,4},{4,5},{5,6},{6,7},{7,8},{8,9},{9,10},{10,1... | collective-permute-start | bytes 49160 | tf_op jit(solution)/shard_map/ppermute | solution.py:551
  11.1 1.3 %collective-permute-start.1 = (f32[16,256]{1,0:T(8,128)}, f32[16,256]{1,0:T(8,128)}, u32[]{:S(2)}, u32[]{:S(2)}) collective-permute-start(f32[16,256]{1,0:T(8,128)} %get-tuple-element.28), channel_id=1, source_target_pairs={{1,0},{2,1},{3,2},{4,3},{5,4},{6,5},{7,6},{8,7},{9,8},{10,9},{11,1... | collective-permute-start | bytes 49160 | tf_op jit(solution)/shard_map/ppermute | solution.py:552
  12.4 7.9 %near.1 = (f32[8,16,256]{2,1,0:T(8,128)}, bf16[896,64]{1,0:T(8,128)(2,1)}, bf16[896,64]{1,0:T(8,128)(2,1)}, bf16[2,256,256]{2,1,0:T(8,128)(2,1)}, bf16[2,256,256]{2,1,0:T(8,128)(2,1)}) custom-call(s32[1]{0:T(128)} %bitcast.me_ref, s32[3,8]{1,0:T(4,128)} %bitcast.12, f32[8,16,256]{2,1,0:T(8,128)} %get-tuple-element.24.refs_1_, f32[4,2,64,64]{3,2,1,0:T(8,128)} %refs_1_.1, ...), custom_call_target="tpu_custom_call" | custom-call | flops 3000000000 | bytes 12000000 | tf_op jit(solution)/shard_map/near/pallas_call | solution.py:558
  20.3 0.0 collective-permute-done.below_hbm.refs_9_
  20.3 0.0 collective-permute-done.1.above_hbm.refs_10_
  20.3 0.0 all-to-all-done.group_hbm.refs_3_
  20.3 2.2 %middle.1 = (f32[344,128]{1,0:T(8,128)}, f32[1,7,8,128]{3,2,1,0:T(8,128)}) custom-call(s32[1]{0:T(128)} %bitcast.me_ref, f32[8,72,128]{2,1,0:T(8,128)} %all-to-all-done.group_hbm.refs_3_, bf16[896,64]{1,0:T(8,128)(2,1)} %get-tuple-element.25.up_high_hbm, bf16[896,64]{1,0:T(8,128)(2,1)} %get-tuple-element.26.up_low_hbm, ...), custom_call_target="tpu_custom_call" | custom-call | tf_op jit(solution)/shard_map/middle/pallas_call | solution.py:610
  22.5 6.1 %collective-permute-start.3 = (f32[1,7,8,128]{3,2,1,0:T(8,128)}, f32[1,7,8,128]{3,2,1,0:T(8,128)}, u32[]{:S(2)}, u32[]{:S(2)}) collective-permute-start(f32[1,7,8,128]{3,2,1,0:T(8,128)} %get-tuple-element.29.refs_0_), channel_id=1, source_target_pairs={{16,0},{17,1},{18,2},{19,3},{20,4},{21,5},{22,6},{23,7},{24,8},{25... | collective-permute-start | bytes 86024 | tf_op jit(solution)/shard_map/ppermute | solution.py:634
  28.6 1.3 %collective-permute-start.2 = (f32[1,7,8,128]{3,2,1,0:T(8,128)}, f32[1,7,8,128]{3,2,1,0:T(8,128)}, u32[]{:S(2)}, u32[]{:S(2)}) collective-permute-start(f32[1,7,8,128]{3,2,1,0:T(8,128)} %get-tuple-element.29.refs_0_), channel_id=1, source_target_pairs={{8,0},{9,1},{10,2},{11,3},{28,4},{29,5},{30,6},{31,7},{16,8},{17,9... | collective-permute-start | bytes 86024 | tf_op jit(solution)/shard_map/ppermute | solution.py:634
  30.0 0.7 %collective-permute-start.4 = (f32[344,128]{1,0:T(8,128)}, f32[344,128]{1,0:T(8,128)}, u32[]{:S(2)}, u32[]{:S(2)}) collective-permute-start(f32[344,128]{1,0:T(8,128)} %get-tuple-element.30), channel_id=1, source_target_pairs={{24,0},{25,1},{26,2},{27,3},{12,4},{13,5},{14,6},{15,7},{0,8},{1,9... | collective-permute-start | bytes 528392 | tf_op jit(solution)/shard_map/ppermute | solution.py:634
  30.6 4.2 %weights.1 = (bf16[576,128]{1,0:T(8,128)(2,1)}, bf16[576,128]{1,0:T(8,128)(2,1)}, bf16[4,576,128]{2,1,0:T(8,128)(2,1)}, bf16[4,576,128]{2,1,0:T(8,128)(2,1)}, bf...) custom-call(s32[1]{0:T(128)} %bitcast.me_ref, s32[4,4]{1,0:T(4,128)} %bitcast.13, ...), custom_call_target="tpu_custom_call" | custom-call | flops 3000000000 | bytes 12000000 | tf_op jit(solution)/shard_map/weights/pallas_call | solution.py:558
  34.9 0.0 collective-permute-done.3.refs_2_
  34.9 0.0 collective-permute-done.2.refs_1_
  34.9 2.6 %collective-permute-done.4.refs_4_ = f32[344,128]{1,0:T(8,128)} collective-permute-done((f32[344,128]{1,0:T(8,128)}, f32[344,128]{1,0:T(8,128)}, u32[]{:S(2)}, u32[]{:S(2)}) %collective-permute-start.4) | collective-permute-done | bytes 176160 | tf_op jit(solution)/shard_map/ppermute | solution.py:634
  37.5 4.9 %down.1 = f32[16,2048]{1,0:T(8,128)} custom-call(s32[1]{0:T(128)} %bitcast.me_ref, f32[1,7,8,128]{3,2,1,0:T(8,128)} %get-tuple-element.29.refs_0_, f32[1,7,8,128]{3,2,1,0:T(8,128)} %collective-permute-done.2.refs_1_, f32[1,7,8,128]{3,2,1,0:T(8,128)} %collective-permute-done.3.refs_2_, f32[8,72,128]{2,1,0:T(8,128)} %all-to-all-done.group_hbm.refs_3_, ...), custom_call_target="tpu_custom_call" | custom-call | tf_op jit(solution)/shard_map/down/pallas_call | solution.py:661
Async XLA Ops:
  2.9 17.4 %all-to-all-start = ((f32[8,72,128]{2,1,0:T(8,128)}), f32[8,72,128]{2,1,0:T(8,128)}, u32[]{:S(2)}, u32[]{:S(2)}) async-start(f32[8,72,128]{2,1,0:T(8,128)} %get-tuple-element.23), calls=%async_computation | async-start | bytes 589824 | tf_op jit(solution)/shard_map/all_to_all | solution.py:549
  8.1 12.2 %collective-permute-start = (f32[16,256]{1,0:T(8,128)}, f32[16,256]{1,0:T(8,128)}, u32[]{:S(2)}, u32[]{:S(2)}) collective-permute-start(f32[16,256]{1,0:T(8,128)} %get-tuple-element.27), channel_id=1, source_target_pairs={{0,1},{1,2},{2,3},{3,4},{4,5},{5,6},{6,7},{7,8},{8,9},{9,10},{10,1... | collective-permute-start | bytes 49160 | tf_op jit(solution)/shard_map/ppermute | solution.py:551
  11.1 9.2 %collective-permute-start.1 = (f32[16,256]{1,0:T(8,128)}, f32[16,256]{1,0:T(8,128)}, u32[]{:S(2)}, u32[]{:S(2)}) collective-permute-start(f32[16,256]{1,0:T(8,128)} %get-tuple-element.28), channel_id=1, source_target_pairs={{1,0},{2,1},{3,2},{4,3},{5,4},{6,5},{7,6},{8,7},{9,8},{10,9},{11,1... | collective-permute-start | bytes 49160 | tf_op jit(solution)/shard_map/ppermute | solution.py:552
  22.5 12.4 %collective-permute-start.3 = (f32[1,7,8,128]{3,2,1,0:T(8,128)}, f32[1,7,8,128]{3,2,1,0:T(8,128)}, u32[]{:S(2)}, u32[]{:S(2)}) collective-permute-start(f32[1,7,8,128]{3,2,1,0:T(8,128)} %get-tuple-element.29.refs_0_), channel_id=1, source_target_pairs={{16,0},{17,1},{18,2},{19,3},{20,4},{21,5},{22,6},{23,7},{24,8},{25... | collective-permute-start | bytes 86024 | tf_op jit(solution)/shard_map/ppermute | solution.py:634
  28.6 6.3 %collective-permute-start.2 = (f32[1,7,8,128]{3,2,1,0:T(8,128)}, f32[1,7,8,128]{3,2,1,0:T(8,128)}, u32[]{:S(2)}, u32[]{:S(2)}) collective-permute-start(f32[1,7,8,128]{3,2,1,0:T(8,128)} %get-tuple-element.29.refs_0_), channel_id=1, source_target_pairs={{8,0},{9,1},{10,2},{11,3},{28,4},{29,5},{30,6},{31,7},{16,8},{17,9... | collective-permute-start | bytes 86024 | tf_op jit(solution)/shard_map/ppermute | solution.py:634
  30.0 7.6 %collective-permute-start.4 = (f32[344,128]{1,0:T(8,128)}, f32[344,128]{1,0:T(8,128)}, u32[]{:S(2)}, u32[]{:S(2)}) collective-permute-start(f32[344,128]{1,0:T(8,128)} %get-tuple-element.30), channel_id=1, source_target_pairs={{24,0},{25,1},{26,2},{27,3},{12,4},{13,5},{14,6},{15,7},{0,8},{1,9... | collective-permute-start | bytes 528392 | tf_op jit(solution)/shard_map/ppermute | solution.py:634
